TPU v7x, 768 devices: a whole 4x8x12 slice. The times are simulated.
768 devices in a mesh: dom: 96 (over y, z), sub: 8 (over x, core).
Axes of the slice: x: 4, y: 8, z: 12, core: 2. Of those that a mesh axis runs over, the one named last changes fastest.
Arguments:
- diagonal: float32 [8, 96, 2, 320, 320], P('sub', 'dom'), may hold values from -1 to 2
- coupling: float32 [8, 96, 2, 3, 80, 80], P('sub', 'dom'), may hold values from -0.25 to 0.25
- start_block: float32 [8, 96, 2, 320, 128], P('sub', 'dom'), may hold values from -25 to 25
- shadow_block: float32 [8, 96, 2, 320, 128], P('sub', 'dom'), may hold values from -25 to 25
Outputs:
- last_basis: float32 [8, 96, 2, 320, 128], P('sub', 'dom')
- last_shadow: float32 [8, 96, 2, 320, 128], P('sub', 'dom')
- moments: float32 [5, 5, 128], replicated
All inputs are finite; a program needn't handle non-finite values.
Results may differ from a plain program's by a relative error of at most 0.0003.
Values sent between devices are 32-bit elements; how exact they have to be, the bound alone decides.
A program may use at most 64 MiB of HBM per device.

v0:
```python
import jax
import jax.numpy as jnp
from jax import lax
from jax.sharding import PartitionSpec as P

NVAR = 5
NQ = 4
STEPS = 4


HIGH = lax.Precision.HIGHEST


def extended(shard, sides, width):
    for axis, dim in sides:
        devices, length = (lax.axis_size(axis), shard.shape[dim])
        up = [(i, (i + 1) % devices) for i in range(devices - 1)]
        down = [(j, i) for i, j in up]
        last = lax.slice_in_dim(shard, length - width, length, axis=dim)
        leading = lax.slice_in_dim(shard, 0, width, axis=dim)
        before = lax.ppermute(last, axis, up)
        after = lax.ppermute(leading, axis, down)
        shard = jnp.concatenate([before, shard, after], axis=dim)
    return shard


def passed_along(block, axis, distance):
    devices = range(lax.axis_size(axis))
    route = [(i - distance, i) for i in devices if i - distance in devices]
    return lax.ppermute(block, axis, route)


def layers(source, begin_at, end_at, along_axis):
    return lax.slice_in_dim(source, begin_at, end_at, axis=along_axis)


def place_rows(added, values, node_axis, position):
    position_key = tuple([slice(None)] * node_axis + [position])
    return added.at[position_key].add(values)


def upper_terms(blocks, next_low):
    return jnp.einsum("xyzfg,sxyzgn->sxyzfn", blocks, next_low, precision=HIGH)


def lower_terms(blocks, high_face):
    return -jnp.einsum("xyzgf,sxyzgn->sxyzfn", blocks, high_face, precision=HIGH)


def edge_terms(edge_block, traces):
    return -jnp.einsum("abgf,sabgn->sabfn", edge_block, traces, precision=HIGH)


def trade_x(first_low, outgoing):
    received = extended(jnp.stack([first_low, outgoing], axis=1), (("sub", 1),), 1)
    return (received[:, 0], received[:, 3])


def trade_y(first_low, outgoing):
    received = extended(jnp.stack([first_low, outgoing], axis=1), (("dom", 1),), 1)
    return (received[:, 0], received[:, 3])


def remote_terms(low_face, high_face, blocks, grid_axis, edge_block, transfer):
    layer_count = low_face.shape[grid_axis]
    outgoing = lax.index_in_dim(high_face, layer_count - 1, grid_axis, keepdims=False)
    product = lower_terms(
        layers(blocks, 0, layer_count - 1, grid_axis - 1),
        layers(high_face, 0, layer_count - 1, grid_axis),
    )
    first_low = lax.index_in_dim(low_face, 0, grid_axis, keepdims=False)
    from_before, from_after = transfer(first_low, outgoing)
    from_before = edge_terms(edge_block, from_before)
    next_low = jnp.concatenate(
        [layers(low_face, 1, layer_count, grid_axis), jnp.expand_dims(from_after, grid_axis)],
        axis=grid_axis,
    )
    lower_rows = jnp.concatenate([jnp.expand_dims(from_before, grid_axis), product], axis=grid_axis)
    return (upper_terms(blocks, next_low), lower_rows)


def apply_pair(stacked, diagonal, coupling, edge_x, edge_y):
    members, count_x, count_y, count_z, size_p, columns = stacked.shape
    node_grid = stacked.reshape(members, count_x, count_y, count_z, NVAR, NQ, NQ, NQ, columns)
    face_size = NVAR * NQ * NQ
    added = jnp.zeros_like(node_grid)
    transfers = [trade_x, trade_y]
    edge_list = [edge_x, edge_y]
    for direction in range(3):
        node_axis = 5 + direction
        grid_axis = 1 + direction
        low_face = lax.index_in_dim(node_grid, 0, node_axis, keepdims=False)
        face_shape = low_face.shape
        low_face = low_face.reshape(members, count_x, count_y, count_z, face_size, columns)
        high_face = lax.index_in_dim(node_grid, NQ - 1, node_axis, keepdims=False).reshape(
            low_face.shape
        )
        blocks = coupling[:, :, :, direction]
        if direction < 2:
            upper_rows, lower_rows = remote_terms(
                low_face, high_face, blocks, grid_axis, edge_list[direction], transfers[direction]
            )
        else:
            zero_layer = jnp.zeros_like(layers(low_face, 0, 1, grid_axis))
            next_low = jnp.concatenate(
                [layers(low_face, 1, count_z, grid_axis), zero_layer], axis=grid_axis
            )
            upper_rows = upper_terms(blocks, next_low)
            product = lower_terms(
                layers(blocks, 0, count_z - 1, grid_axis - 1),
                layers(high_face, 0, count_z - 1, grid_axis),
            )
            lower_rows = jnp.concatenate([zero_layer, product], axis=grid_axis)
        added = place_rows(added, upper_rows.reshape(face_shape), node_axis, NQ - 1)
        added = place_rows(added, lower_rows.reshape(face_shape), node_axis, 0)
    face_part = added.reshape(stacked.shape)
    forward = jnp.einsum("xyzpq,xyzqn->xyzpn", diagonal, stacked[0], precision=HIGH) + face_part[0]
    backward = jnp.einsum("xyzqp,xyzqn->xyzpn", diagonal, stacked[1], precision=HIGH) - face_part[1]
    return jnp.stack([forward, backward])


def local_moments(shadow_list, basis_list, inverse_total):
    return (
        jnp.einsum(
            "ixyzpn,jxyzpn->ijn", jnp.stack(shadow_list), jnp.stack(basis_list), precision=HIGH
        )
        * inverse_total
    )


def body(diagonal, coupling, start_block, shadow_block):
    count_x, count_y, count_z, size_p, columns = start_block.shape
    inverse_total = 1.0 / (
        count_x * count_y * count_z * size_p * lax.axis_size("sub") * lax.axis_size("dom")
    )
    edge_x = None
    edge_y = None
    edge_x = passed_along(coupling[count_x - 1, :, :, 0], "sub", 1)
    edge_y = passed_along(coupling[:, count_y - 1, :, 1], "dom", 1)
    basis_list = [start_block]
    shadow_list = [shadow_block]
    stacked = jnp.stack([start_block, shadow_block])
    for step_index in range(STEPS):
        stacked = apply_pair(stacked, diagonal, coupling, edge_x, edge_y)
        basis_list.append(stacked[0])
        shadow_list.append(stacked[1])
    moments = lax.psum(local_moments(shadow_list, basis_list, inverse_total), ("dom", "sub"))
    return (stacked[0], stacked[1], moments)


def solution(mesh):
    placed = (
        P("sub", "dom", None, None, None),
        P("sub", "dom", None, None, None, None),
        P("sub", "dom", None, None, None),
        P("sub", "dom", None, None, None),
    )
    return jax.shard_map(
        body,
        mesh=mesh,
        in_specs=placed,
        out_specs=(P("sub", "dom", None, None, None), P("sub", "dom", None, None, None), P()),
        check_vma=False,
    )
```

profile of v0, /device:TPU:1, one launch (start us, length us, event | category | flops | bytes accessed | tf_op | source)
XLA Modules:
  0.0 289.1 jit_solution(11608092575262112136)
XLA Ops:
  0.7 1.1 slice_bitcast_fusion.8
  1.8 4.8 %collective-permute-start.5 = (f32[1,2,80,80]{3,2,1,0:T(8,128)S(1)}, f32[1,2,80,80]{3,2,1,0:T(8,128)S(1)}, u32[]{:S(2)}, u32[]{:S(2)}) collective-permute-start(f32[1,2,80,80]{3,2,1,0:T(8,128)S(1)} %get-tuple-element.327), channel_id=1, source_target_pairs={{0,8},{8,16},{16,24},{24,32},{32,40},{40,48},{48,56},{56,64},{64,7... | collective-permute-start | bytes 153608 | tf_op jit(solution)/shard_map/ppermute | solution.py:30
  6.6 4.0 %collective-permute-start.2 = (f32[1,2,80,80]{3,2,1,0:T(8,128)S(1)}, f32[1,2,80,80]{3,2,1,0:T(8,128)S(1)}, u32[]{:S(2)}, u32[]{:S(2)}) collective-permute-start(f32[1,2,80,80]{3,2,1,0:T(8,128)S(1)} %get-tuple-element.328), channel_id=1, source_target_pairs={{0,1},{1,2},{2,3},{3,4},{4,5},{5,6},{6,7},{8,9},{9,10},{10,11},{11... | collective-permute-start | bytes 153608 | tf_op jit(solution)/shard_map/ppermute | solution.py:30
  10.6 1.1 fusion.41
  11.7 1.3 collective-permute-start.3
  13.0 4.6 %collective-permute-start.4 = (f32[2,1,1,2,80,128]{5,4,0,3,2,1:T(8,128)S(1)}, f32[2,1,1,2,80,128]{5,4,0,3,2,1:T(8,128)S(1)}, u32[]{:S(2)}, u32[]{:S(2)}) collective-permute-start(f32[2,1,1,2,80,128]{5,4,0,3,2,1:T(8,128)S(1)} %bitcast.505), channel_id=1, source_target_pairs={{0,8},{8,16},{16,24},{24,32},{32,40},{40,48},{48,56},{56,64},{64,7... | collective-permute-start | bytes 491528 | tf_op jit(solution)/shard_map/ppermute | solution.py:21
  17.8 6.1 %collective-permute-start = (f32[2,1,1,2,80,128]{5,4,0,3,2,1:T(8,128)S(1)}, f32[2,1,1,2,80,128]{5,4,0,3,2,1:T(8,128)S(1)}, u32[]{:S(2)}, u32[]{:S(2)}) collective-permute-start(f32[2,1,1,2,80,128]{5,4,0,3,2,1:T(8,128)S(1)} %bitcast.513), channel_id=1, source_target_pairs={{1,0},{2,1},{3,2},{4,3},{5,4},{6,5},{7,6},{9,8},{10,9},{11,10},{12... | collective-permute-start | bytes 491528 | tf_op jit(solution)/shard_map/ppermute | solution.py:22
  24.2 0.8 bitcast_dynamic-update-slice_fusion.9
  25.0 0.8 bitcast_dynamic-update-slice_fusion.4
  26.4 1.9 collective-permute-start.1
  28.3 0.3 fusion.80
  28.8 1.8 collective-permute-done.1
  30.6 0.3 convolution_negate_fusion.7
  31.4 0.3 convolution_negate_fusion.6
  32.1 6.1 %scatter-add.86 = f32[2,1,1,2,5,4,4,4,128]{8,7,6,5,4,3,2,1,0:T(4,128)S(1)} dynamic-update-slice(f32[2,1,1,2,5,4,4,4,128]{8,7,6,5,4,3,2,1,0:T(4,128)S(1)} %fusion.48, f32[2,1,1,2,5,4,4,1,128]{8,7,6,5,4,3,2,1,0:T(1,128)S(1)} %slice_add_fusion.13, s32[]{:T(128)} %constant.515.clone.1, s32[]{:T(128)} %constant.515.clone.1, s32[]{:T(128)} %constant.515.clone.1, s32[]{:T(128)} %constant.515.clone.1, ...) | dynamic-update-slice | bytes 327684 | tf_op jit(solution)/shard_map/scatter-add | solution.py:39
  38.4 6.1 %scatter-add.89 = f32[2,1,1,2,5,4,4,4,128]{8,7,6,5,4,3,2,1,0:T(4,128)S(1)} dynamic-update-slice(f32[2,1,1,2,5,4,4,4,128]{8,7,6,5,4,3,2,1,0:T(4,128)S(1)} %scatter-add.86, f32[2,1,1,2,5,4,4,1,128]{8,7,6,5,4,3,2,1,0:T(1,128)S(1)} %slice_add_fusion.12, s32[]{:T(128)} %constant.515.clone.1, s32[]{:T(128)} %constant.515.clone.1, s32[]{:T(128)} %constant.515.clone.1, s32[]{:T(128)} %constant.515.clone.1, ...) | dynamic-update-slice | bytes 327684 | tf_op jit(solution)/shard_map/scatter-add | solution.py:39
  44.5 1.7 bitcast_dynamic-update-slice_fusion.8
  46.2 2.6 bitcast_dynamic-update-slice_fusion.3
  49.3 1.3 collective-permute-start.8
  50.6 4.0 %collective-permute-start.9 = (f32[2,1,1,2,80,128]{5,4,0,3,2,1:T(8,128)S(1)}, f32[2,1,1,2,80,128]{5,4,0,3,2,1:T(8,128)S(1)}, u32[]{:S(2)}, u32[]{:S(2)}) collective-permute-start(f32[2,1,1,2,80,128]{5,4,0,3,2,1:T(8,128)S(1)} %bitcast.508), channel_id=1, source_target_pairs={{0,8},{8,16},{16,24},{24,32},{32,40},{40,48},{48,56},{56,64},{64,7... | collective-permute-start | bytes 491528 | tf_op jit(solution)/shard_map/ppermute | solution.py:21
  55.0 1.9 collective-permute-start.6
  57.0 5.1 %collective-permute-start.7 = (f32[2,1,1,2,80,128]{5,4,0,3,2,1:T(8,128)S(1)}, f32[2,1,1,2,80,128]{5,4,0,3,2,1:T(8,128)S(1)}, u32[]{:S(2)}, u32[]{:S(2)}) collective-permute-start(f32[2,1,1,2,80,128]{5,4,0,3,2,1:T(8,128)S(1)} %bitcast.516), channel_id=1, source_target_pairs={{0,1},{1,2},{2,3},{3,4},{4,5},{5,6},{6,7},{8,9},{9,10},{10,11},{11... | collective-permute-start | bytes 491528 | tf_op jit(solution)/shard_map/ppermute | solution.py:21
  62.4 0.6 collective-permute-done.6
  63.4 0.7 collective-permute-done.7
  64.2 0.3 convolution_negate_fusion.5
  64.5 0.3 fusion.69
  65.0 0.3 convolution_negate_fusion.4
  65.7 6.1 %scatter-add.96 = f32[2,1,1,2,5,4,4,4,128]{8,7,6,5,4,3,2,1,0:T(4,128)S(1)} dynamic-update-slice(f32[2,1,1,2,5,4,4,4,128]{8,7,6,5,4,3,2,1,0:T(4,128)S(1)} %fusion.46, f32[2,1,1,2,5,4,4,1,128]{8,7,6,5,4,3,2,1,0:T(1,128)S(1)} %slice_add_fusion.9, s32[]{:T(128)} %constant.515.clone.1, s32[]{:T(128)} %constant.515.clone.1, s32[]{:T(128)} %constant.515.clone.1, s32[]{:T(128)} %constant.515.clone.1, ...) | dynamic-update-slice | bytes 327684 | tf_op jit(solution)/shard_map/scatter-add | solution.py:39
  72.0 6.1 %scatter-add.99 = f32[2,1,1,2,5,4,4,4,128]{8,7,6,5,4,3,2,1,0:T(4,128)S(1)} dynamic-update-slice(f32[2,1,1,2,5,4,4,4,128]{8,7,6,5,4,3,2,1,0:T(4,128)S(1)} %scatter-add.96, f32[2,1,1,2,5,4,4,1,128]{8,7,6,5,4,3,2,1,0:T(1,128)S(1)} %slice_add_fusion.8, s32[]{:T(128)} %constant.515.clone.1, s32[]{:T(128)} %constant.515.clone.1, s32[]{:T(128)} %constant.515.clone.1, s32[]{:T(128)} %constant.515.clone.1, ...) | dynamic-update-slice | bytes 327684 | tf_op jit(solution)/shard_map/scatter-add | solution.py:39
  78.1 2.7 bitcast_dynamic-update-slice_fusion.2
  80.8 1.7 bitcast_dynamic-update-slice_fusion.7
  83.0 1.3 collective-permute-start.12
  84.3 4.2 %collective-permute-start.13 = (f32[2,1,1,2,80,128]{5,4,0,3,2,1:T(8,128)S(1)}, f32[2,1,1,2,80,128]{5,4,0,3,2,1:T(8,128)S(1)}, u32[]{:S(2)}, u32[]{:S(2)}) collective-permute-start(f32[2,1,1,2,80,128]{5,4,0,3,2,1:T(8,128)S(1)} %bitcast.509), channel_id=1, source_target_pairs={{0,8},{8,16},{16,24},{24,32},{32,40},{40,48},{48,56},{56,64},{64,7... | collective-permute-start | bytes 491528 | tf_op jit(solution)/shard_map/ppermute | solution.py:21
  88.9 1.9 collective-permute-start.10
  90.8 4.9 %collective-permute-start.11 = (f32[2,1,1,2,80,128]{5,4,0,3,2,1:T(8,128)S(1)}, f32[2,1,1,2,80,128]{5,4,0,3,2,1:T(8,128)S(1)}, u32[]{:S(2)}, u32[]{:S(2)}) collective-permute-start(f32[2,1,1,2,80,128]{5,4,0,3,2,1:T(8,128)S(1)} %bitcast.517), channel_id=1, source_target_pairs={{0,1},{1,2},{2,3},{3,4},{4,5},{5,6},{6,7},{8,9},{9,10},{10,11},{11... | collective-permute-start | bytes 491528 | tf_op jit(solution)/shard_map/ppermute | solution.py:21
  96.0 0.6 collective-permute-done.10
  96.6 0.3 fusion.64
  97.1 0.7 collective-permute-done.11
  97.8 0.3 convolution_negate_fusion.3
  98.2 0.3 fusion.61
  98.6 0.3 convolution_negate_fusion.2
  99.3 6.1 %scatter-add.106 = f32[2,1,1,2,5,4,4,4,128]{8,7,6,5,4,3,2,1,0:T(4,128)S(1)} dynamic-update-slice(f32[2,1,1,2,5,4,4,4,128]{8,7,6,5,4,3,2,1,0:T(4,128)S(1)} %fusion.44, f32[2,1,1,2,5,4,4,1,128]{8,7,6,5,4,3,2,1,0:T(1,128)S(1)} %slice_add_fusion.5, s32[]{:T(128)} %constant.515.clone.1, s32[]{:T(128)} %constant.515.clone.1, s32[]{:T(128)} %constant.515.clone.1, s32[]{:T(128)} %constant.515.clone.1, ...) | dynamic-update-slice | bytes 327684 | tf_op jit(solution)/shard_map/scatter-add | solution.py:39
  105.6 6.1 %scatter-add.109 = f32[2,1,1,2,5,4,4,4,128]{8,7,6,5,4,3,2,1,0:T(4,128)S(1)} dynamic-update-slice(f32[2,1,1,2,5,4,4,4,128]{8,7,6,5,4,3,2,1,0:T(4,128)S(1)} %scatter-add.106, f32[2,1,1,2,5,4,4,1,128]{8,7,6,5,4,3,2,1,0:T(1,128)S(1)} %slice_add_fusion.4, s32[]{:T(128)} %constant.515.clone.1, s32[]{:T(128)} %constant.515.clone.1, s32[]{:T(128)} %constant.515.clone.1, s32[]{:T(128)} %constant.515.clone.1, ...) | dynamic-update-slice | bytes 327684 | tf_op jit(solution)/shard_map/scatter-add | solution.py:39
  111.7 2.7 bitcast_dynamic-update-slice_fusion.1
  114.4 1.7 bitcast_dynamic-update-slice_fusion.6
  116.6 1.3 collective-permute-start.16
  117.9 5.2 %collective-permute-start.17 = (f32[2,1,1,2,80,128]{5,4,0,3,2,1:T(8,128)S(1)}, f32[2,1,1,2,80,128]{5,4,0,3,2,1:T(8,128)S(1)}, u32[]{:S(2)}, u32[]{:S(2)}) collective-permute-start(f32[2,1,1,2,80,128]{5,4,0,3,2,1:T(8,128)S(1)} %bitcast.507), channel_id=1, source_target_pairs={{0,8},{8,16},{16,24},{24,32},{32,40},{40,48},{48,56},{56,64},{64,7... | collective-permute-start | bytes 491528 | tf_op jit(solution)/shard_map/ppermute | solution.py:21
  123.4 1.9 collective-permute-start.14
  125.4 4.9 %collective-permute-start.15 = (f32[2,1,1,2,80,128]{5,4,0,3,2,1:T(8,128)S(1)}, f32[2,1,1,2,80,128]{5,4,0,3,2,1:T(8,128)S(1)}, u32[]{:S(2)}, u32[]{:S(2)}) collective-permute-start(f32[2,1,1,2,80,128]{5,4,0,3,2,1:T(8,128)S(1)} %bitcast.515), channel_id=1, source_target_pairs={{0,1},{1,2},{2,3},{3,4},{4,5},{5,6},{6,7},{8,9},{9,10},{10,11},{11... | collective-permute-start | bytes 491528 | tf_op jit(solution)/shard_map/ppermute | solution.py:21
  130.6 0.6 collective-permute-done.14
  131.1 0.3 fusion.56
  131.6 0.7 collective-permute-done.15
  132.3 0.3 convolution_negate_fusion.1
  132.7 0.3 fusion.53
  133.1 0.3 convolution_negate_fusion
  133.8 6.1 %scatter-add.116 = f32[2,1,1,2,5,4,4,4,128]{8,7,6,5,4,3,2,1,0:T(4,128)S(1)} dynamic-update-slice(f32[2,1,1,2,5,4,4,4,128]{8,7,6,5,4,3,2,1,0:T(4,128)S(1)} %fusion.42, f32[2,1,1,2,5,4,4,1,128]{8,7,6,5,4,3,2,1,0:T(1,128)S(1)} %slice_add_fusion.1, s32[]{:T(128)} %constant.515.clone.1, s32[]{:T(128)} %constant.515.clone.1, s32[]{:T(128)} %constant.515.clone.1, s32[]{:T(128)} %constant.515.clone.1, ...) | dynamic-update-slice | bytes 327684 | tf_op jit(solution)/shard_map/scatter-add | solution.py:39
  140.1 6.1 %scatter-add.119 = f32[2,1,1,2,5,4,4,4,128]{8,7,6,5,4,3,2,1,0:T(4,128)S(1)} dynamic-update-slice(f32[2,1,1,2,5,4,4,4,128]{8,7,6,5,4,3,2,1,0:T(4,128)S(1)} %scatter-add.116, f32[2,1,1,2,5,4,4,1,128]{8,7,6,5,4,3,2,1,0:T(1,128)S(1)} %slice_add_fusion, s32[]{:T(128)} %constant.515.clone.1, s32[]{:T(128)} %constant.515.clone.1, s32[]{:T(128)} %constant.515.clone.1, s32[]{:T(128)} %constant.515.clone.1, ...) | dynamic-update-slice | bytes 327684 | tf_op jit(solution)/shard_map/scatter-add | solution.py:39
  146.3 1.8 bitcast_dynamic-update-slice_fusion.5
  148.1 3.5 %copy.74 = f32[5,2,320,128]{2,0,1,3:T(8,128)} copy(f32[5,2,320,128]{3,2,1,0:T(8,128)} %bitcast.462) | data formatting | bytes 3276800 | tf_op jit(solution)/shard_map/reshape.1513
  151.6 2.7 bitcast_dynamic-update-slice_fusion
  154.3 2.3 copy.75
  156.6 8.5 %fusion.1 = f32[5,5,128]{0,1,2:T(8,128)S(1)} fusion(f32[5,2,320,128]{2,0,1,3:T(8,128)} %copy.74, f32[5,2,320,128]{2,0,1,3:T(8,128)} %copy.75), kind=kOutput, calls=%fused_computation.2 | convolution fusion | flops 24579200 | bytes 3289600 | tf_op jit(solution)/shard_map/ixyzpn,jxyzpn->ijn/dot_general | solution.py:124
  165.1 123.2 %psum.7 = f32[5,5,128]{0,1,2:T(8,128)S(1)} all-reduce(f32[5,5,128]{0,1,2:T(8,128)S(1)} %fusion.1), channel_id=1, replica_groups=mesh['dom'=96,'sub'=8] {'dom','sub'}, use_global_device_ids=true, to_apply=%region_0.0 | all-reduce | flops 3200 | bytes 25600 | tf_op jit(solution)/shard_map/psum | solution.py:147
  288.3 0.8 copy.76
  (106 shorter events, 8.1 us)
Async XLA Ops:
  0.6 43.9 %copy-start = (f32[1,1,2,320,320]{4,3,2,1,0:T(8,128)S(1)}, f32[1,1,2,320,320]{4,3,2,1,0:T(8,128)}, u32[]{:S(2)}) copy-start(f32[1,1,2,320,320]{4,3,2,1,0:T(8,128)} %param.52) | copy-start | bytes 2457604
  0.6 17.0 %copy-start.2 = (f32[1,1,2,320,128]{4,3,2,1,0:T(8,128)S(1)}, f32[1,1,2,320,128]{4,3,2,1,0:T(8,128)}, u32[]{:S(2)}) copy-start(f32[1,1,2,320,128]{4,3,2,1,0:T(8,128)} %param.55) | copy-start | bytes 983044
  0.7 17.0 %copy-start.1 = (f32[1,1,2,320,128]{4,3,2,1,0:T(8,128)S(1)}, f32[1,1,2,320,128]{4,3,2,1,0:T(8,128)}, u32[]{:S(2)}) copy-start(f32[1,1,2,320,128]{4,3,2,1,0:T(8,128)} %param.54) | copy-start | bytes 983044
  1.8 29.6 %collective-permute-start.5 = (f32[1,2,80,80]{3,2,1,0:T(8,128)S(1)}, f32[1,2,80,80]{3,2,1,0:T(8,128)S(1)}, u32[]{:S(2)}, u32[]{:S(2)}) collective-permute-start(f32[1,2,80,80]{3,2,1,0:T(8,128)S(1)} %get-tuple-element.327), channel_id=1, source_target_pairs={{0,8},{8,16},{16,24},{24,32},{32,40},{40,48},{48,56},{56,64},{64,7... | collective-permute-start | bytes 153608 | tf_op jit(solution)/shard_map/ppermute | solution.py:30
  6.6 22.2 %collective-permute-start.2 = (f32[1,2,80,80]{3,2,1,0:T(8,128)S(1)}, f32[1,2,80,80]{3,2,1,0:T(8,128)S(1)}, u32[]{:S(2)}, u32[]{:S(2)}) collective-permute-start(f32[1,2,80,80]{3,2,1,0:T(8,128)S(1)} %get-tuple-element.328), channel_id=1, source_target_pairs={{0,1},{1,2},{2,3},{3,4},{4,5},{5,6},{6,7},{8,9},{9,10},{10,11},{11... | collective-permute-start | bytes 153608 | tf_op jit(solution)/shard_map/ppermute | solution.py:30
  11.7 19.2 %collective-permute-start.3 = (f32[2,1,1,2,80,128]{5,4,0,3,2,1:T(8,128)S(1)}, f32[2,1,1,2,80,128]{5,4,0,3,2,1:T(8,128)S(1)}, u32[]{:S(2)}, u32[]{:S(2)}) collective-permute-start(f32[2,1,1,2,80,128]{5,4,0,3,2,1:T(8,128)S(1)} %bitcast.506), channel_id=1, source_target_pairs={{8,0},{16,8},{24,16},{32,24},{40,32},{48,40},{56,48},{64,56},{72,6... | collective-permute-start | bytes 491528 | tf_op jit(solution)/shard_map/ppermute | solution.py:22
  13.0 18.3 %collective-permute-start.4 = (f32[2,1,1,2,80,128]{5,4,0,3,2,1:T(8,128)S(1)}, f32[2,1,1,2,80,128]{5,4,0,3,2,1:T(8,128)S(1)}, u32[]{:S(2)}, u32[]{:S(2)}) collective-permute-start(f32[2,1,1,2,80,128]{5,4,0,3,2,1:T(8,128)S(1)} %bitcast.505), channel_id=1, source_target_pairs={{0,8},{8,16},{16,24},{24,32},{32,40},{40,48},{48,56},{56,64},{64,7... | collective-permute-start | bytes 491528 | tf_op jit(solution)/shard_map/ppermute | solution.py:21
  17.8 8.6 %collective-permute-start = (f32[2,1,1,2,80,128]{5,4,0,3,2,1:T(8,128)S(1)}, f32[2,1,1,2,80,128]{5,4,0,3,2,1:T(8,128)S(1)}, u32[]{:S(2)}, u32[]{:S(2)}) collective-permute-start(f32[2,1,1,2,80,128]{5,4,0,3,2,1:T(8,128)S(1)} %bitcast.513), channel_id=1, source_target_pairs={{1,0},{2,1},{3,2},{4,3},{5,4},{6,5},{7,6},{9,8},{10,9},{11,10},{12... | collective-permute-start | bytes 491528 | tf_op jit(solution)/shard_map/ppermute | solution.py:22
  24.2 1.9 copy-start.3
  26.4 4.2 %collective-permute-start.1 = (f32[2,1,1,2,80,128]{5,4,0,3,2,1:T(8,128)S(1)}, f32[2,1,1,2,80,128]{5,4,0,3,2,1:T(8,128)S(1)}, u32[]{:S(2)}, u32[]{:S(2)}) collective-permute-start(f32[2,1,1,2,80,128]{5,4,0,3,2,1:T(8,128)S(1)} %bitcast.514), channel_id=1, source_target_pairs={{0,1},{1,2},{2,3},{3,4},{4,5},{5,6},{6,7},{8,9},{9,10},{10,11},{11... | collective-permute-start | bytes 491528 | tf_op jit(solution)/shard_map/ppermute | solution.py:21
  49.3 15.2 %collective-permute-start.8 = (f32[2,1,1,2,80,128]{5,4,0,3,2,1:T(8,128)S(1)}, f32[2,1,1,2,80,128]{5,4,0,3,2,1:T(8,128)S(1)}, u32[]{:S(2)}, u32[]{:S(2)}) collective-permute-start(f32[2,1,1,2,80,128]{5,4,0,3,2,1:T(8,128)S(1)} %bitcast.511), channel_id=1, source_target_pairs={{8,0},{16,8},{24,16},{32,24},{40,32},{48,40},{56,48},{64,56},{72,6... | collective-permute-start | bytes 491528 | tf_op jit(solution)/shard_map/ppermute | solution.py:22
  50.6 14.3 %collective-permute-start.9 = (f32[2,1,1,2,80,128]{5,4,0,3,2,1:T(8,128)S(1)}, f32[2,1,1,2,80,128]{5,4,0,3,2,1:T(8,128)S(1)}, u32[]{:S(2)}, u32[]{:S(2)}) collective-permute-start(f32[2,1,1,2,80,128]{5,4,0,3,2,1:T(8,128)S(1)} %bitcast.508), channel_id=1, source_target_pairs={{0,8},{8,16},{16,24},{24,32},{32,40},{40,48},{48,56},{56,64},{64,7... | collective-permute-start | bytes 491528 | tf_op jit(solution)/shard_map/ppermute | solution.py:21
  55.0 7.9 %collective-permute-start.6 = (f32[2,1,1,2,80,128]{5,4,0,3,2,1:T(8,128)S(1)}, f32[2,1,1,2,80,128]{5,4,0,3,2,1:T(8,128)S(1)}, u32[]{:S(2)}, u32[]{:S(2)}) collective-permute-start(f32[2,1,1,2,80,128]{5,4,0,3,2,1:T(8,128)S(1)} %bitcast.518), channel_id=1, source_target_pairs={{1,0},{2,1},{3,2},{4,3},{5,4},{6,5},{7,6},{9,8},{10,9},{11,10},{12... | collective-permute-start | bytes 491528 | tf_op jit(solution)/shard_map/ppermute | solution.py:22
  57.0 7.2 %collective-permute-start.7 = (f32[2,1,1,2,80,128]{5,4,0,3,2,1:T(8,128)S(1)}, f32[2,1,1,2,80,128]{5,4,0,3,2,1:T(8,128)S(1)}, u32[]{:S(2)}, u32[]{:S(2)}) collective-permute-start(f32[2,1,1,2,80,128]{5,4,0,3,2,1:T(8,128)S(1)} %bitcast.516), channel_id=1, source_target_pairs={{0,1},{1,2},{2,3},{3,4},{4,5},{5,6},{6,7},{8,9},{9,10},{10,11},{11... | collective-permute-start | bytes 491528 | tf_op jit(solution)/shard_map/ppermute | solution.py:21
  83.0 15.2 %collective-permute-start.12 = (f32[2,1,1,2,80,128]{5,4,0,3,2,1:T(8,128)S(1)}, f32[2,1,1,2,80,128]{5,4,0,3,2,1:T(8,128)S(1)}, u32[]{:S(2)}, u32[]{:S(2)}) collective-permute-start(f32[2,1,1,2,80,128]{5,4,0,3,2,1:T(8,128)S(1)} %bitcast.512), channel_id=1, source_target_pairs={{8,0},{16,8},{24,16},{32,24},{40,32},{48,40},{56,48},{64,56},{72,6... | collective-permute-start | bytes 491528 | tf_op jit(solution)/shard_map/ppermute | solution.py:22
  84.3 14.3 %collective-permute-start.13 = (f32[2,1,1,2,80,128]{5,4,0,3,2,1:T(8,128)S(1)}, f32[2,1,1,2,80,128]{5,4,0,3,2,1:T(8,128)S(1)}, u32[]{:S(2)}, u32[]{:S(2)}) collective-permute-start(f32[2,1,1,2,80,128]{5,4,0,3,2,1:T(8,128)S(1)} %bitcast.509), channel_id=1, source_target_pairs={{0,8},{8,16},{16,24},{24,32},{32,40},{40,48},{48,56},{56,64},{64,7... | collective-permute-start | bytes 491528 | tf_op jit(solution)/shard_map/ppermute | solution.py:21
  88.9 7.7 %collective-permute-start.10 = (f32[2,1,1,2,80,128]{5,4,0,3,2,1:T(8,128)S(1)}, f32[2,1,1,2,80,128]{5,4,0,3,2,1:T(8,128)S(1)}, u32[]{:S(2)}, u32[]{:S(2)}) collective-permute-start(f32[2,1,1,2,80,128]{5,4,0,3,2,1:T(8,128)S(1)} %bitcast.519), channel_id=1, source_target_pairs={{1,0},{2,1},{3,2},{4,3},{5,4},{6,5},{7,6},{9,8},{10,9},{11,10},{12... | collective-permute-start | bytes 491528 | tf_op jit(solution)/shard_map/ppermute | solution.py:22
  90.8 7.0 %collective-permute-start.11 = (f32[2,1,1,2,80,128]{5,4,0,3,2,1:T(8,128)S(1)}, f32[2,1,1,2,80,128]{5,4,0,3,2,1:T(8,128)S(1)}, u32[]{:S(2)}, u32[]{:S(2)}) collective-permute-start(f32[2,1,1,2,80,128]{5,4,0,3,2,1:T(8,128)S(1)} %bitcast.517), channel_id=1, source_target_pairs={{0,1},{1,2},{2,3},{3,4},{4,5},{5,6},{6,7},{8,9},{9,10},{10,11},{11... | collective-permute-start | bytes 491528 | tf_op jit(solution)/shard_map/ppermute | solution.py:21
  116.6 16.1 %collective-permute-start.16 = (f32[2,1,1,2,80,128]{5,4,0,3,2,1:T(8,128)S(1)}, f32[2,1,1,2,80,128]{5,4,0,3,2,1:T(8,128)S(1)}, u32[]{:S(2)}, u32[]{:S(2)}) collective-permute-start(f32[2,1,1,2,80,128]{5,4,0,3,2,1:T(8,128)S(1)} %bitcast.510), channel_id=1, source_target_pairs={{8,0},{16,8},{24,16},{32,24},{40,32},{48,40},{56,48},{64,56},{72,6... | collective-permute-start | bytes 491528 | tf_op jit(solution)/shard_map/ppermute | solution.py:22
  117.9 15.2 %collective-permute-start.17 = (f32[2,1,1,2,80,128]{5,4,0,3,2,1:T(8,128)S(1)}, f32[2,1,1,2,80,128]{5,4,0,3,2,1:T(8,128)S(1)}, u32[]{:S(2)}, u32[]{:S(2)}) collective-permute-start(f32[2,1,1,2,80,128]{5,4,0,3,2,1:T(8,128)S(1)} %bitcast.507), channel_id=1, source_target_pairs={{0,8},{8,16},{16,24},{24,32},{32,40},{40,48},{48,56},{56,64},{64,7... | collective-permute-start | bytes 491528 | tf_op jit(solution)/shard_map/ppermute | solution.py:21
  123.4 7.7 %collective-permute-start.14 = (f32[2,1,1,2,80,128]{5,4,0,3,2,1:T(8,128)S(1)}, f32[2,1,1,2,80,128]{5,4,0,3,2,1:T(8,128)S(1)}, u32[]{:S(2)}, u32[]{:S(2)}) collective-permute-start(f32[2,1,1,2,80,128]{5,4,0,3,2,1:T(8,128)S(1)} %bitcast.520), channel_id=1, source_target_pairs={{1,0},{2,1},{3,2},{4,3},{5,4},{6,5},{7,6},{9,8},{10,9},{11,10},{12... | collective-permute-start | bytes 491528 | tf_op jit(solution)/shard_map/ppermute | solution.py:22
  125.4 6.9 %collective-permute-start.15 = (f32[2,1,1,2,80,128]{5,4,0,3,2,1:T(8,128)S(1)}, f32[2,1,1,2,80,128]{5,4,0,3,2,1:T(8,128)S(1)}, u32[]{:S(2)}, u32[]{:S(2)}) collective-permute-start(f32[2,1,1,2,80,128]{5,4,0,3,2,1:T(8,128)S(1)} %bitcast.515), channel_id=1, source_target_pairs={{0,1},{1,2},{2,3},{3,4},{4,5},{5,6},{6,7},{8,9},{9,10},{10,11},{11... | collective-permute-start | bytes 491528 | tf_op jit(solution)/shard_map/ppermute | solution.py:21
  148.1 3.5 %copy-start.4 = (f32[5,1,1,2,320,128]{5,4,3,2,1,0:T(8,128)S(1)}, f32[5,1,1,2,320,128]{5,4,3,2,1,0:T(8,128)}, u32[]{:S(2)}) copy-start(f32[5,1,1,2,320,128]{5,4,3,2,1,0:T(8,128)} %get-tuple-element.341) | copy-start | bytes 4915204
where the time goes:
time: 295 us; the launch traced here: 289 us
  blocking collectives  123 us (42%)
  starting transfers between devices  60.8 us (21%)
  local copies, waits for them, and re-layouts  59.2 us (20%)
  matrix products  33.2 us (11%)
  waiting for transfers between devices  5.72 us (2%)
  other arithmetic  5.29 us (2%)
    psum x1, blocking collectives, body(): lax.psum(local_moments(shadow_list, basis_list, inverse_total), ('dom', '...  123 us
    scatter-add x16, local copies, waits for them, and re-layouts, place_rows(): return added.at[position_key].add(values)  49.2 us
    ppermute x8, starting transfers between devices, extended(): before = lax.ppermute(last, axis, up)  34.9 us
    ppermute x8, starting transfers between devices, extended(): after = lax.ppermute(leading, axis, down)  17.1 us
    dot_general x4, matrix products, apply_pair(): jnp.einsum('xyzqp,xyzqn->xyzpn', diagonal, stacked[1], precision=HIGH)  10.6 us
    ppermute x2, starting transfers between devices, passed_along(): return lax.ppermute(block, axis, route)  8.79 us
    dot_general x1, matrix products, local_moments(): jnp.einsum('ixyzpn,jxyzpn->ijn', jnp.stack(shadow_list), jnp.stack(basis_...  8.51 us
    dot_general x4, matrix products, apply_pair(): jnp.einsum('xyzpq,xyzqn->xyzpn', diagonal, stacked[0], precision=HIGH)  6.93 us
  transfers between devices with their start and end apart: 18, of which 7 were waited for; matrix products, arithmetic and copies ran while one was open for 3% of the time, Pallas kernels for 0%

commit v1 on v0

v1 whole, which is shorter than its diff:
```python
import functools

import jax
import jax.numpy as jnp
from jax import lax
from jax.experimental import pallas as pl
from jax.experimental.pallas import tpu as pltpu
from jax.sharding import PartitionSpec as P

STEPS = 4
ROWS = 320
FACE = 80
COLS = 128
MESH = pl.DeviceIdType.MESH
F32 = jnp.float32
BF16 = jnp.bfloat16
X_DOWN, Y_DOWN, X_UP, Y_UP = range(4)


def split(x):
    high = x.astype(BF16)
    return high, (x - high.astype(F32)).astype(BF16)


def put_columns(ref, row, x):
    high, low = split(x)
    rows = pl.ds(row, x.shape[0])
    ref[rows, 0:COLS] = high
    ref[rows, COLS:] = low


def put_rows(ref, row, column, below, x):
    high, low = split(x)
    columns = pl.ds(column, x.shape[1])
    ref[pl.ds(row, x.shape[0]), columns] = high
    ref[pl.ds(row + below, x.shape[0]), columns] = low


def product(left, right):
    full = jnp.dot(left, right, preferred_element_type=F32)
    rows = full.shape[0] // 2
    return full[:rows, :COLS] + (full[:rows, COLS:] + full[rows:, :COLS])


def low_half(shape):
    return lax.broadcasted_iota(jnp.int32, shape, len(shape) - 2) < 4


def swap_halves(x):
    return pltpu.roll(x, 4, 1)


def x_trace(u, node):
    return u.reshape(2, 5, 64, COLS)[:, :, node * 16 : node * 16 + 16].reshape(2, FACE, COLS)


def y_low(u):
    parts = u.reshape(20, 4, 8, COLS)
    first, second = parts[:, 0], parts[:, 2]
    return jnp.where(low_half(first.shape), first, swap_halves(second)).reshape(2, FACE, COLS)


def y_high(u):
    parts = u.reshape(20, 4, 8, COLS)
    first, second = parts[:, 1], parts[:, 3]
    return jnp.where(low_half(first.shape), swap_halves(first), second).reshape(2, FACE, COLS)


def scattered(x_lo, y_lo, x_hi, y_hi):
    x_lo = x_lo.reshape(10, 1, 16, COLS)
    x_hi = x_hi.reshape(10, 1, 16, COLS)
    gap = jnp.zeros((10, 1, 32, COLS), F32)
    along_x = jnp.concatenate([x_lo, gap, x_hi], axis=2).reshape(20, 4, 8, COLS)
    y_lo = y_lo.reshape(20, 8, COLS)
    y_hi = y_hi.reshape(20, 8, COLS)
    mask = low_half(y_lo.shape)
    zero = jnp.zeros_like(y_lo)
    along_y = [
        jnp.where(mask, y_lo, zero),
        jnp.where(mask, zero, swap_halves(y_hi)),
        jnp.where(mask, swap_halves(y_lo), zero),
        jnp.where(mask, zero, y_hi),
    ]
    along_y = jnp.concatenate([part[:, None] for part in along_y], axis=1)
    return (along_x + along_y).reshape(2, ROWS, COLS)


def column_sums(x, y):
    return jnp.sum((x * y).reshape(2 * ROWS, COLS), axis=0, keepdims=True)


def kernel(
    sizes,
    scale,
    d_hbm,
    c_hbm,
    b_hbm,
    s_hbm,
    ob_hbm,
    os_hbm,
    om_ref,
    d_in,
    c_in,
    field,
    acc,
    d_pad,
    c_pad,
    z_pad,
    left,
    left_up,
    left_in,
    right,
    right_up,
    right_in,
    sent,
    got,
    sums,
    sums_got,
    load_sem,
    store_sem,
    send_sem,
    recv_sem,
    sums_send,
    sums_recv,
):
    doms, subs, depth = sizes
    heights = doms // depth
    dom, sub = lax.axis_index("dom"), lax.axis_index("sub")
    height, level = dom // depth, lax.rem(dom, depth)

    loads = [
        pltpu.make_async_copy(c_hbm, c_in, load_sem.at[0]),
        pltpu.make_async_copy(b_hbm, field.at[0], load_sem.at[1]),
        pltpu.make_async_copy(s_hbm, field.at[1], load_sem.at[2]),
        pltpu.make_async_copy(d_hbm, d_in, load_sem.at[3]),
    ]
    for load in loads:
        load.start()

    on_sub = lambda by: (dom, lax.rem(sub + by + subs, subs))
    on_dom = lambda by: (lax.rem(dom + by + doms, doms), sub)
    on_level = lambda by: (height * depth + lax.rem(level + by, depth), sub)
    on_height = lambda by: (lax.rem(height + by, heights) * depth + level, sub)
    stages = [
        [on_sub(by) for by in range(1, subs)],
        [on_height(by) for by in range(1, heights)],
        [on_level(by) for by in range(1, depth)],
    ]
    sides = [on_sub(-1), on_dom(-1), on_sub(1), on_dom(1)]
    greeted = [on_dom(-1), on_dom(1)] + stages[0] + stages[1] + stages[2]
    barrier = pltpu.get_barrier_semaphore()
    for peer in greeted:
        pl.semaphore_signal(barrier, inc=1, device_id=peer, device_id_type=MESH)

    for ref in (c_pad, z_pad, d_pad):
        ref[...] = jnp.zeros_like(ref)
    for ref in (left, left_up, left_in, right, right_up, right_in):
        ref[...] = jnp.zeros_like(ref)

    loads[0].wait()
    coupling = c_in[...]
    keep_x = jnp.where(sub == subs - 1, 0.0, 1.0)
    keep_y = jnp.where(dom == doms - 1, 0.0, 1.0)
    c_pad[:, 0, 0:FACE, 0:FACE] = coupling[:, 0] * keep_x
    c_pad[:, 1, 0:FACE, 0:FACE] = coupling[:, 1] * keep_y
    c_pad[:, 2, 0:FACE, 0:FACE] = coupling[:, 2]
    for e in range(2):
        for side in range(2):
            block = c_pad[e, side]
            put_rows(left_in.at[e], side * FACE, side * COLS, 2 * FACE, block[:FACE])
            put_rows(left_up.at[e], side * FACE, side * COLS, 2 * FACE, block.T[:FACE])

    def messages(k, f):
        return [
            pltpu.make_async_remote_copy(
                src_ref=sent.at[k, f, side],
                dst_ref=got.at[k, f, side],
                send_sem=send_sem.at[k, f, side],
                recv_sem=recv_sem.at[k, f, side],
                device_id=peer,
                device_id_type=MESH,
            )
            for side, peer in enumerate(sides)
        ]

    def send_faces(k, f, u):
        copies = messages(k, f)
        sent[k, f, X_DOWN] = x_trace(u, 0)
        copies[X_DOWN].start()
        sent[k, f, Y_DOWN] = y_low(u)
        copies[Y_DOWN].start()
        x_hi, y_hi = x_trace(u, 3), y_high(u)
        for e in range(2):
            put_columns(right_up.at[e], 0, x_hi[e])
            put_columns(right_up.at[e], COLS, y_hi[e])
        for e in range(2):
            up = product(left_up[e], right_up[e])
            sent[k, f, X_UP, e] = up[:FACE]
            sent[k, f, Y_UP, e] = up[FACE:]
        copies[Y_UP].start()
        copies[X_UP].start()

    def local_part(f):
        for e in range(2):
            put_columns(right.at[e], 0, field[f, e])
            put_columns(right.at[e], 384, field[f, 1 - e, pl.ds(3 * e, FACE, stride=4), :])
        for e in range(2):
            acc[f, e] = product(left[f, e], right[e])

    def face_part(k, f):
        for copy in messages(k, f):
            copy.wait_recv()
        for e in range(2):
            put_columns(right_in.at[e], 0, got[k, f, X_DOWN, e])
            put_columns(right_in.at[e], COLS, got[k, f, Y_DOWN, e])
        into = [product(left_in[e], right_in[e]) for e in range(2)]
        x_hi = jnp.concatenate([part[None, :FACE] for part in into], axis=0)
        y_hi = jnp.concatenate([part[None, FACE:] for part in into], axis=0)
        terms = scattered(-got[k, f, X_UP], -got[k, f, Y_UP], x_hi, y_hi)
        return acc[f] + terms if f == 0 else acc[f] - terms

    def total_copies(group, stage):
        first = sum(len(peers) for peers in stages[:stage])
        return [
            pltpu.make_async_remote_copy(
                src_ref=sums.at[group, stage],
                dst_ref=sums_got.at[group, first + i],
                send_sem=sums_send.at[group, first + i],
                recv_sem=sums_recv.at[group, first + i],
                device_id=peer,
                device_id_type=MESH,
            )
            for i, peer in enumerate(stages[stage])
        ]

    def start_total(group, stage):
        for copy in total_copies(group, stage):
            copy.start()

    def end_total(group, stage):
        first = sum(len(peers) for peers in stages[:stage])
        copies = total_copies(group, stage)
        for copy in copies:
            copy.wait_recv()
        total = sums[group, stage]
        for i in range(len(copies)):
            total = total + sums_got[group, first + i]
        sums[group, stage + 1] = total

    pl.semaphore_wait(barrier, len(greeted))

    for f in range(2):
        loads[1 + f].wait()
        send_faces(0, f, field[f])
    sums[...] = jnp.zeros_like(sums)
    sums[0, 0, 0:1] = column_sums(field[1], field[0])

    loads[3].wait()
    z_pad[0, pl.ds(3, FACE, stride=4), :] = c_pad[0, 2, 0:FACE]
    z_pad[1, pl.ds(0, FACE, stride=4), :] = -c_pad[0, 2].T[:FACE]
    for e in range(2):
        d_pad[e, 0:ROWS, 0:ROWS] = d_in[e]
        put_rows(left.at[0, e], 0, 0, ROWS, d_pad[e, 0:ROWS, :])
        put_rows(left.at[0, e], 0, 384, ROWS, z_pad[e])
        put_rows(left.at[1, e], 0, 384, ROWS, -z_pad[e])
        for i in range(3):
            rows = min(COLS, ROWS - i * COLS)
            for j in range(3):
                block = d_pad[e, j * COLS : (j + 1) * COLS, i * COLS : (i + 1) * COLS].T
                put_rows(left.at[1, e], i * COLS, j * COLS, ROWS, block[:rows])
    for f in range(2):
        local_part(f)

    for k in range(STEPS):
        for f in range(2):
            u = face_part(k, f)
            field[f] = u
            if k + 1 < STEPS:
                send_faces(k + 1, f, u)
                local_part(f)
            else:
                pltpu.make_async_copy(field.at[f], (ob_hbm, os_hbm)[f], store_sem.at[f]).start()
            moment = 2 * k + 1 + f
            group, row = (0, moment) if moment < 7 else (1, moment - 7)
            sums[group, 0, row : row + 1] = column_sums(field[1], field[0])
            if moment == 6:
                start_total(0, 0)
            if moment == 7:
                end_total(0, 0)
                start_total(0, 1)
    start_total(1, 0)
    end_total(0, 1)
    start_total(0, 2)
    end_total(1, 0)
    start_total(1, 1)
    end_total(0, 2)
    end_total(1, 1)
    start_total(1, 2)
    end_total(1, 2)
    early, late = sums[0, 3] * scale, sums[1, 3] * scale
    rows = [early[i : i + 1] for i in range(7)] + [late[i : i + 1] for i in range(2)]
    for i in range(STEPS + 1):
        for j in range(STEPS + 1):
            om_ref[i, j : j + 1] = rows[i + j]

    for k in range(STEPS):
        for f in range(2):
            for copy in messages(k, f):
                copy.wait_send()
    for group in range(2):
        for stage in range(3):
            for copy in total_copies(group, stage):
                copy.wait_send()
    for f in range(2):
        pltpu.make_async_copy(field.at[f], (ob_hbm, os_hbm)[f], store_sem.at[f]).wait()


def solution(mesh):
    doms, subs = mesh.shape["dom"], mesh.shape["sub"]
    depth = 12 if doms % 12 == 0 else 1
    peers = (subs - 1) + (doms // depth - 1) + (depth - 1)

    def body(diagonal, coupling, start_block, shadow_block):
        count = 2 * ROWS * doms * subs
        moments_shape = (STEPS + 1, STEPS + 1, COLS)
        field_shape = jax.ShapeDtypeStruct((2, ROWS, COLS), F32)
        outs = pl.pallas_call(
            functools.partial(kernel, (doms, subs, depth), 1.0 / count),
            out_shape=(field_shape, field_shape, jax.ShapeDtypeStruct(moments_shape, F32)),
            in_specs=[pl.BlockSpec(memory_space=pltpu.HBM)] * 4,
            out_specs=(
                pl.BlockSpec(memory_space=pltpu.HBM),
                pl.BlockSpec(memory_space=pltpu.HBM),
                pl.BlockSpec(memory_space=pltpu.VMEM),
            ),
            scratch_shapes=[
                pltpu.VMEM((2, ROWS, ROWS), F32),
                pltpu.VMEM((2, 3, FACE, FACE), F32),
                pltpu.VMEM((2, 2, ROWS, COLS), F32),
                pltpu.VMEM((2, 2, ROWS, COLS), F32),
                pltpu.VMEM((2, 384, 384), F32),
                pltpu.VMEM((2, 3, COLS, COLS), F32),
                pltpu.VMEM((2, ROWS, COLS), F32),
                pltpu.VMEM((2, 2, 2 * ROWS, 512), BF16),
                pltpu.VMEM((2, 4 * FACE, 256), BF16),
                pltpu.VMEM((2, 4 * FACE, 256), BF16),
                pltpu.VMEM((2, 512, 256), BF16),
                pltpu.VMEM((2, 256, 256), BF16),
                pltpu.VMEM((2, 256, 256), BF16),
                pltpu.VMEM((STEPS, 2, 4, 2, FACE, COLS), F32),
                pltpu.VMEM((STEPS, 2, 4, 2, FACE, COLS), F32),
                pltpu.VMEM((2, 4, 8, COLS), F32),
                pltpu.VMEM((2, peers, 8, COLS), F32),
                pltpu.SemaphoreType.DMA((4,)),
                pltpu.SemaphoreType.DMA((2,)),
                pltpu.SemaphoreType.DMA((STEPS, 2, 4)),
                pltpu.SemaphoreType.DMA((STEPS, 2, 4)),
                pltpu.SemaphoreType.DMA((2, peers)),
                pltpu.SemaphoreType.DMA((2, peers)),
            ],
            compiler_params=pltpu.CompilerParams(
                collective_id=0, has_side_effects=True, vmem_limit_bytes=40 * 1024 * 1024
            ),
            name="powers",
        )(
            diagonal.reshape(2, ROWS, ROWS),
            coupling.reshape(2, 3, FACE, FACE),
            start_block.reshape(2, ROWS, COLS),
            shadow_block.reshape(2, ROWS, COLS),
        )
        shape = start_block.shape
        return outs[0].reshape(shape), outs[1].reshape(shape), outs[2]

    placed = P("sub", "dom", None, None, None)
    return jax.shard_map(
        body,
        mesh=mesh,
        in_specs=(placed, P("sub", "dom", None, None, None, None), placed, placed),
        out_specs=(placed, placed, P()),
        check_vma=False,
    )
```

time: 295 us -> 67.7 us (0.23); the launches traced: 289 us -> 66.5 us
  blocking collectives: 123 us -> 0 us
  starting transfers between devices: 60.8 us -> 0 us
  Pallas kernels: 0 us -> 59.8 us
  local copies, waits for them, and re-layouts: 59.2 us -> 6.14 us
  matrix products: 33.2 us -> 0 us
  waiting for transfers between devices: 5.72 us -> 0 us
  other arithmetic: 5.29 us -> 0 us
    psum x1 -> x0, blocking collectives: 123 us -> none  [body(): lax.psum(local_moments(shadow_list, basis_list, inverse_total), ('dom', '...]
    ppermute x18 -> x0, starting transfers between devices: 60.8 us -> none  [the longest x8 34.9 us: extended(): before = lax.ppermute(last, axis, up)]
    pallas_call x0 -> x1, Pallas kernels: none -> 59.8 us  [body(): pl.pallas_call(functools.partial(kernel, (doms, subs, depth), 1.0 / count...]
    scatter-add x16 -> x0, local copies, waits for them, and re-layouts: 49.2 us -> none  [place_rows(): return added.at[position_key].add(values)]
    dot_general x33 -> x0, matrix products: 33.2 us -> none  [the longest x4 10.6 us: apply_pair(): jnp.einsum('xyzqp,xyzqn->xyzpn', diagonal, stacked[1], precision=HIGH)]
    another operation x2 -> x0, local copies, waits for them, and re-layouts: 5.86 us -> none
    ppermute x18 -> x0, waiting for transfers between devices: 5.72 us -> none  [the longest x8 3.92 us: extended(): before = lax.ppermute(last, axis, up)]
    unnamed x15 -> x11, local copies, waits for them, and re-layouts: 2.41 us -> 6.14 us
  transfers between devices with their start and end apart: 18 -> 0, of which waited for: 7 -> 0; matrix products, arithmetic and copies ran while one was open for 3% -> 0% of each run, Pallas kernels for 0% -> 0%
where the time goes in v1:
time: 67.7 us; the launch traced here: 66.5 us
  Pallas kernels  59.8 us (88%)
  local copies, waits for them, and re-layouts  6.14 us (9%)
    pallas_call x1, Pallas kernels, body(): pl.pallas_call(functools.partial(kernel, (doms, subs, depth), 1.0 / count...  59.8 us
    unnamed x11, local copies, waits for them, and re-layouts  6.14 us

profile of v1, /device:TPU:1, one launch (start us, length us, event | category | flops | bytes accessed | tf_op | source)
XLA Modules:
  0.0 66.5 jit_solution(3931686408973525164)
XLA Ops:
  0.6 0.0 copy-start
  0.6 1.2 %copy-done = f32[1,1,2,320,320]{4,3,2,1,0:T(8,128)S(1)} copy-done((f32[1,1,2,320,320]{4,3,2,1,0:T(8,128)S(1)}, f32[1,1,2,320,320]{4,3,2,1,0:T(8,128)}, u32[]{:S(2)}) %copy-start) | copy-done | bytes 819224
  1.8 0.0 copy-start.1
  1.8 1.0 %copy-done.1 = f32[1,1,2,320,128]{4,3,2,1,0:T(8,128)S(1)} copy-done((f32[1,1,2,320,128]{4,3,2,1,0:T(8,128)S(1)}, f32[1,1,2,320,128]{4,3,2,1,0:T(8,128)}, u32[]{:S(2)}) %copy-start.1) | copy-done | bytes 327704
  2.8 0.0 copy-start.2
  2.8 1.0 %copy-done.2 = f32[1,1,2,320,128]{4,3,2,1,0:T(8,128)S(1)} copy-done((f32[1,1,2,320,128]{4,3,2,1,0:T(8,128)S(1)}, f32[1,1,2,320,128]{4,3,2,1,0:T(8,128)}, u32[]{:S(2)}) %copy-start.2) | copy-done | bytes 327704
  3.8 0.0 copy-start.3
  3.8 0.9 %copy-done.3 = f32[1,1,2,3,80,80]{5,4,3,2,1,0:T(8,128)S(1)} copy-done((f32[1,1,2,3,80,80]{5,4,3,2,1,0:T(8,128)S(1)}, f32[1,1,2,3,80,80]{5,4,3,2,1,0:T(8,128)}, u32[]{:S(2)}) %copy-start.3) | copy-done | bytes 153624
  4.7 59.8 %powers.1 = (f32[2,320,128]{2,1,0:T(8,128)S(1)}, f32[2,320,128]{2,1,0:T(8,128)S(1)}, f32[5,5,128]{2,1,0:T(8,128)S(1)}) custom-call(f32[2,320,320]{2,1,0:T(8,128)S(1)} %bitcast.6, f32[2,3,80,80]{3,2,1,0:T(8,128)S(1)} %bitcast.11, f32[2,320,128]{2,1,0:T(8,128)S(1)} %bitcast.7, f32[2,320,128]{2,1,0:T(8,128)S(1)} %bitcast.8), custom_call_target="tpu_custom_call" | custom-call | tf_op jit(solution)/shard_map/powers/pallas_call | solution.py:327
  64.5 0.7 %copy.10 = f32[1,1,2,320,128]{4,3,2,1,0:T(8,128)} copy(f32[1,1,2,320,128]{4,3,2,1,0:T(8,128)S(1)} %bitcast.10) | data formatting | bytes 655360
  65.2 0.7 %copy.11 = f32[1,1,2,320,128]{4,3,2,1,0:T(8,128)} copy(f32[1,1,2,320,128]{4,3,2,1,0:T(8,128)S(1)} %bitcast.9) | data formatting | bytes 655360
  65.9 0.6 copy.12
Async XLA Ops:
  0.6 1.2 %copy-start = (f32[1,1,2,320,320]{4,3,2,1,0:T(8,128)S(1)}, f32[1,1,2,320,320]{4,3,2,1,0:T(8,128)}, u32[]{:S(2)}) copy-start(f32[1,1,2,320,320]{4,3,2,1,0:T(8,128)} %param.4) | copy-start | bytes 2457604
  1.8 1.0 %copy-start.1 = (f32[1,1,2,320,128]{4,3,2,1,0:T(8,128)S(1)}, f32[1,1,2,320,128]{4,3,2,1,0:T(8,128)}, u32[]{:S(2)}) copy-start(f32[1,1,2,320,128]{4,3,2,1,0:T(8,128)} %param.6) | copy-start | bytes 983044
  2.8 1.0 %copy-start.2 = (f32[1,1,2,320,128]{4,3,2,1,0:T(8,128)S(1)}, f32[1,1,2,320,128]{4,3,2,1,0:T(8,128)}, u32[]{:S(2)}) copy-start(f32[1,1,2,320,128]{4,3,2,1,0:T(8,128)} %param.7) | copy-start | bytes 983044
  3.8 0.9 %copy-start.3 = (f32[1,1,2,3,80,80]{5,4,3,2,1,0:T(8,128)S(1)}, f32[1,1,2,3,80,80]{5,4,3,2,1,0:T(8,128)}, u32[]{:S(2)}) copy-start(f32[1,1,2,3,80,80]{5,4,3,2,1,0:T(8,128)} %param.5) | copy-start | bytes 460804

commit v2 on v1

v2 whole, which is shorter than its diff:
```python
import functools

import jax
import jax.numpy as jnp
from jax import lax
from jax.experimental import pallas as pl
from jax.experimental.pallas import tpu as pltpu
from jax.sharding import PartitionSpec as P

STEPS = 4
ROWS = 320
FACE = 80
COLS = 128
MESH = pl.DeviceIdType.MESH
F32 = jnp.float32
BF16 = jnp.bfloat16
X_DOWN, Y_DOWN, X_UP, Y_UP = range(4)
TOKENS = 6
SUMS = 2 * STEPS + 1


def split(x):
    high = x.astype(BF16)
    return high, (x - high.astype(F32)).astype(BF16)


def put_columns(ref, row, x):
    high, low = split(x)
    rows = pl.ds(row, x.shape[0])
    ref[rows, 0:COLS] = high
    ref[rows, COLS:] = low


def put_rows(ref, row, column, below, x):
    high, low = split(x)
    columns = pl.ds(column, x.shape[1])
    ref[pl.ds(row, x.shape[0]), columns] = high
    ref[pl.ds(row + below, x.shape[0]), columns] = low


def product(left, right):
    full = jnp.dot(left, right, preferred_element_type=F32)
    rows = full.shape[0] // 2
    return full[:rows, :COLS] + (full[:rows, COLS:] + full[rows:, :COLS])


def x_face(ref, node):
    return ref[:, :, node * 16 : node * 16 + 16].reshape(2, FACE, COLS)


def low_half(shape):
    return lax.broadcasted_iota(jnp.int32, shape, len(shape) - 2) < 4


def swap_halves(x):
    return pltpu.roll(x, 4, 1)


def y_parts(u):
    parts = u.reshape(20, 4, 8, COLS)
    return [parts[:, i] for i in range(4)]


def y_low(u):
    first, _, second, _ = y_parts(u)
    return jnp.where(low_half(first.shape), first, swap_halves(second)).reshape(2, FACE, COLS)


def y_high(u):
    _, first, _, second = y_parts(u)
    return jnp.where(low_half(first.shape), swap_halves(first), second).reshape(2, FACE, COLS)


def add_y(u, low, high):
    parts = y_parts(u)
    low, high = low.reshape(20, 8, COLS), high.reshape(20, 8, COLS)
    mask = low_half(low.shape)
    zero = jnp.zeros_like(low)
    terms = [
        jnp.where(mask, low, zero),
        jnp.where(mask, zero, swap_halves(high)),
        jnp.where(mask, swap_halves(low), zero),
        jnp.where(mask, zero, high),
    ]
    whole = jnp.concatenate([(part + term)[:, None] for part, term in zip(parts, terms)], axis=1)
    return whole.reshape(2, 5, 64, COLS)


def column_sums(x, y):
    return jnp.sum((x * y).reshape(2 * ROWS, COLS), axis=0, keepdims=True)


def far_first(count):
    return sorted(range(1, count), key=lambda by: -min(by, count - by))


def kernel(
    sizes,
    d_hbm,
    c_hbm,
    b_hbm,
    s_hbm,
    ob_hbm,
    os_hbm,
    total_ref,
    d_in,
    c_in,
    field,
    acc,
    d_pad,
    c_pad,
    z_pad,
    left,
    left_up,
    left_in,
    right,
    right_up,
    right_in,
    sent,
    got,
    sums,
    sums_got,
    load_sem,
    store_sem,
    send_sem,
    recv_sem,
    sums_send,
    sums_recv,
    token_sem,
):
    doms, subs, depth = sizes
    heights, chips = doms // depth, subs // 2
    dom, sub = lax.axis_index("dom"), lax.axis_index("sub")
    height, level = dom // depth, lax.rem(dom, depth)
    chip, core = sub // 2, lax.rem(sub, 2)

    loads = [
        pltpu.make_async_copy(b_hbm, field.at[0], load_sem.at[0]),
        pltpu.make_async_copy(c_hbm, c_in, load_sem.at[1]),
        pltpu.make_async_copy(s_hbm, field.at[1], load_sem.at[2]),
        pltpu.make_async_copy(d_hbm, d_in, load_sem.at[3]),
    ]
    for load in loads:
        load.start()

    def on_sub(by):
        return dom, lax.rem(sub + by + subs, subs)

    def on_dom(by):
        return lax.rem(dom + by + doms, doms), sub

    def on_level(by, to=sub):
        return height * depth + lax.rem(level + by + depth, depth), to

    def on_height(by):
        return lax.rem(height + by + heights, heights) * depth + level, sub

    def on_chip(by, to):
        return dom, lax.rem(chip + by, chips) * 2 + to

    sides = [on_sub(-1), on_dom(-1), on_sub(1), on_dom(1)]
    near = [on_level(-1), on_level(1), on_height(-1), on_height(1)]
    barrier = pltpu.get_barrier_semaphore()
    for peer in sides + near:
        pl.semaphore_signal(barrier, inc=1, device_id=peer, device_id_type=MESH)

    def pass_token(step):
        for peer in near:
            pl.semaphore_signal(token_sem.at[step], inc=1, device_id=peer, device_id_type=MESH)

    def message(k, f, side):
        return pltpu.make_async_remote_copy(
            src_ref=sent.at[k, f, side],
            dst_ref=got.at[k, f, side],
            send_sem=send_sem.at[k, f, side],
            recv_sem=recv_sem.at[k, f, side],
            device_id=sides[side],
            device_id_type=MESH,
        )

    def through(lefts, side, rights, x):
        for e in range(2):
            put_columns(rights.at[side, e], 0, x[e])
        parts = [product(lefts[side, e], rights[side, e]) for e in range(2)]
        return jnp.concatenate([part[None] for part in parts], axis=0)

    for ref in (c_pad, right_up, right_in):
        ref[...] = jnp.zeros_like(ref)

    loads[0].wait()
    sent[0, 0, Y_DOWN] = y_low(field[0])
    sent[0, 0, X_DOWN] = x_face(field.at[0], 0)
    pl.semaphore_wait(barrier, len(sides + near))
    message(0, 0, Y_DOWN).start()
    message(0, 0, X_DOWN).start()
    pass_token(0)

    loads[1].wait()
    for e in range(2):
        for side, last in enumerate((sub == subs - 1, dom == doms - 1)):
            c_pad[e, side, 0:FACE, 0:FACE] = jnp.where(last, 0.0, c_in[e, side])
        c_pad[e, 2, 0:FACE, 0:FACE] = c_in[e, 2]
    for side in (1, 0):
        for e in range(2):
            put_rows(left_up.at[side, e], 0, 0, FACE, c_pad[e, side].T[:FACE])

    def send_up(k, f, side, trace):
        sent[k, f, X_UP + side] = through(left_up, side, right_up, trace)
        message(k, f, X_UP + side).start()

    send_up(0, 0, 1, y_high(field[0]))
    send_up(0, 0, 0, x_face(field.at[0], 3))
    loads[2].wait()
    sent[0, 1, Y_DOWN] = y_low(field[1])
    message(0, 1, Y_DOWN).start()
    send_up(0, 1, 1, y_high(field[1]))
    sent[0, 1, X_DOWN] = x_face(field.at[1], 0)
    message(0, 1, X_DOWN).start()
    send_up(0, 1, 0, x_face(field.at[1], 3))

    for side in range(2):
        for e in range(2):
            put_rows(left_in.at[side, e], 0, 0, FACE, c_pad[e, side, 0:FACE])
    for ref in (z_pad, d_pad, left, right):
        ref[...] = jnp.zeros_like(ref)
    z_pad[0, pl.ds(3, FACE, stride=4), :] = c_pad[0, 2, 0:FACE]
    z_pad[1, pl.ds(0, FACE, stride=4), :] = -c_pad[0, 2].T[:FACE]
    loads[3].wait()
    for e in range(2):
        d_pad[e, 0:ROWS, 0:ROWS] = d_in[e]
        put_rows(left.at[0, e], 0, 0, ROWS, d_pad[e, 0:ROWS, :])
        put_rows(left.at[0, e], 0, 384, ROWS, z_pad[e])
        put_rows(left.at[1, e], 0, 384, ROWS, -z_pad[e])
        for i in range(3):
            rows = min(COLS, ROWS - i * COLS)
            for j in range(3):
                block = d_pad[e, j * COLS : (j + 1) * COLS, i * COLS : (i + 1) * COLS].T
                put_rows(left.at[1, e], i * COLS, j * COLS, ROWS, block[:rows])

    def local_part(f):
        flat = field.at[f].reshape(2, ROWS, COLS)
        for e in range(2):
            put_columns(right.at[e], 0, flat[e])
            put_columns(right.at[e], 384, flat[1 - e, pl.ds(3 * e, FACE, stride=4), :])
        for e in range(2):
            acc[f, e] = product(left[f, e], right[e]).reshape(5, 64, COLS)

    for f in range(2):
        local_part(f)
    sums[0, 0:1] = column_sums(field[1], field[0])

    for k in range(STEPS):
        for f in range(2):
            more = k + 1 < STEPS
            sign = 1.0 - 2.0 * f
            message(k, f, X_UP).wait_recv()
            message(k, f, X_DOWN).wait_recv()
            into = through(left_in, 0, right_in, got[k, f, X_DOWN]).reshape(2, 5, 16, COLS)
            acc[f, :, :, 48:64] = acc[f, :, :, 48:64] + sign * into
            from_below = got[k, f, X_UP].reshape(2, 5, 16, COLS)
            acc[f, :, :, 0:16] = acc[f, :, :, 0:16] - sign * from_below
            u = acc[f]
            message(k, f, Y_UP).wait_recv()
            low = -sign * got[k, f, Y_UP]
            if more:
                sent[k + 1, f, Y_DOWN] = y_low(u) + low
                message(k + 1, f, Y_DOWN).start()
            message(k, f, Y_DOWN).wait_recv()
            high = sign * through(left_in, 1, right_in, got[k, f, Y_DOWN])
            if more:
                send_up(k + 1, f, 1, y_high(u) + high)
            field[f] = add_y(u, low, high)
            if more:
                sent[k + 1, f, X_DOWN] = x_face(field.at[f], 0)
                message(k + 1, f, X_DOWN).start()
                send_up(k + 1, f, 0, x_face(field.at[f], 3))
                local_part(f)
            else:
                pltpu.make_async_copy(field.at[f], (ob_hbm, os_hbm)[f], store_sem.at[f]).start()
            moment = 2 * k + 1 + f
            sums[0, moment : moment + 1] = column_sums(field[1], field[0])
            step = 2 * k + f
            if step < TOKENS:
                pl.semaphore_wait(token_sem.at[step], len(near))
                if step + 1 < TOKENS:
                    pass_token(step + 1)

    def total_copy(stage, slot, peer, send=None):
        return pltpu.make_async_remote_copy(
            src_ref=sums.at[stage],
            dst_ref=sums_got.at[slot],
            send_sem=sums_send.at[slot if send is None else send],
            recv_sem=sums_recv.at[slot],
            device_id=peer,
            device_id_type=MESH,
        )

    def arrived(total, stage, first, count):
        for slot in range(first, first + count):
            total_copy(stage, slot, on_level(1)).wait_recv()
            total = total + sums_got[slot]
        return total

    inner, outer = on_chip(0, 0), on_chip(0, 1)
    across = far_first(chips)
    slot_in, slot_y = 2 * len(across), 2 * len(across) + 1
    slot_z = slot_y + heights - 1
    slot_out = slot_z + depth - 1

    @pl.when(core == 0)
    def _():
        copies = [total_copy(0, i, on_chip(by, 1)) for i, by in enumerate(across)]
        copies.append(total_copy(0, slot_in, outer))
        for copy in copies:
            copy.start()
        total_copy(2, slot_out, outer).wait_recv()
        total_ref[...] = arrived(sums_got[slot_out], 2, slot_z, depth - 1)
        for copy in copies:
            copy.wait_send()

    @pl.when(core == 1)
    def _():
        copies = [total_copy(0, len(across) + i, on_chip(by, 1)) for i, by in enumerate(across)]
        for copy in copies:
            copy.start()
        sums[1] = arrived(sums[0], 0, 0, slot_y)
        along_y = [total_copy(1, slot_y + i, on_height(by)) for i, by in enumerate(far_first(heights))]
        for copy in along_y:
            copy.start()
        sums[2] = arrived(sums[1], 1, slot_y, heights - 1)
        along_z = []
        for i, by in enumerate(far_first(depth)):
            along_z.append(total_copy(2, slot_z + i, on_level(by, chip * 2), slot_out + 1 + i))
            along_z.append(total_copy(2, slot_z + i, on_level(by)))
        along_z.append(total_copy(2, slot_out, inner))
        for copy in along_z:
            copy.start()
        total_ref[...] = arrived(sums[2], 2, slot_z, depth - 1)
        for copy in copies + along_y + along_z:
            copy.wait_send()

    for k in range(STEPS):
        for f in range(2):
            for side in range(4):
                message(k, f, side).wait_send()
    for f in range(2):
        pltpu.make_async_copy(field.at[f], (ob_hbm, os_hbm)[f], store_sem.at[f]).wait()


def pin(x):
    return pltpu.with_memory_space_constraint(x, pltpu.HBM)


def finish(scale, b_hbm, s_hbm, total_ref, ob_hbm, os_hbm, moments_ref, sem):
    copies = [
        pltpu.make_async_copy(b_hbm, ob_hbm, sem.at[0]),
        pltpu.make_async_copy(s_hbm, os_hbm, sem.at[1]),
    ]
    for copy in copies:
        copy.start()
    total = total_ref[...] * scale
    for i in range(STEPS + 1):
        moments_ref[i] = total[i : i + STEPS + 1]
    for copy in copies:
        copy.wait()


def solution(mesh):
    doms, subs = mesh.shape["dom"], mesh.shape["sub"]
    depth = 12
    slots = 2 * (subs // 2 - 1) + 1 + (doms // depth - 1) + (depth - 1) + 1
    anywhere = pl.BlockSpec(memory_space=pl.ANY)
    inside = pl.BlockSpec(memory_space=pltpu.VMEM)
    grant = 40 * 1024 * 1024

    def body(diagonal, coupling, start_block, shadow_block):
        count = 2 * ROWS * doms * subs
        field_shape = jax.ShapeDtypeStruct((2, 5, 64, COLS), F32)
        moments_shape = jax.ShapeDtypeStruct((STEPS + 1, STEPS + 1, COLS), F32)
        total_shape = jax.ShapeDtypeStruct((SUMS, COLS), F32)
        powers = pl.pallas_call(
            functools.partial(kernel, (doms, subs, depth)),
            out_shape=(field_shape, field_shape, total_shape),
            in_specs=[anywhere] * 4,
            out_specs=(anywhere, anywhere, inside),
            scratch_shapes=[
                pltpu.VMEM((2, ROWS, ROWS), F32),
                pltpu.VMEM((2, 3, FACE, FACE), F32),
                pltpu.VMEM((2, 2, 5, 64, COLS), F32),
                pltpu.VMEM((2, 2, 5, 64, COLS), F32),
                pltpu.VMEM((2, 384, 384), F32),
                pltpu.VMEM((2, 3, COLS, COLS), F32),
                pltpu.VMEM((2, ROWS, COLS), F32),
                pltpu.VMEM((2, 2, 2 * ROWS, 512), BF16),
                pltpu.VMEM((2, 2, 2 * FACE, COLS), BF16),
                pltpu.VMEM((2, 2, 2 * FACE, COLS), BF16),
                pltpu.VMEM((2, 512, 256), BF16),
                pltpu.VMEM((2, 2, COLS, 256), BF16),
                pltpu.VMEM((2, 2, COLS, 256), BF16),
                pltpu.VMEM((STEPS, 2, 4, 2, FACE, COLS), F32),
                pltpu.VMEM((STEPS, 2, 4, 2, FACE, COLS), F32),
                pltpu.VMEM((3, SUMS, COLS), F32),
                pltpu.VMEM((slots, SUMS, COLS), F32),
                pltpu.SemaphoreType.DMA((4,)),
                pltpu.SemaphoreType.DMA((2,)),
                pltpu.SemaphoreType.DMA((STEPS, 2, 4)),
                pltpu.SemaphoreType.DMA((STEPS, 2, 4)),
                pltpu.SemaphoreType.DMA((slots + depth - 1,)),
                pltpu.SemaphoreType.DMA((slots,)),
                pltpu.SemaphoreType.REGULAR((TOKENS,)),
            ],
            compiler_params=pltpu.CompilerParams(
                collective_id=0, has_side_effects=True, vmem_limit_bytes=grant
            ),
            name="powers",
        )(
            pin(diagonal.reshape(2, ROWS, ROWS)),
            pin(coupling.reshape(2, 3, FACE, FACE)),
            pin(start_block.reshape(2, 5, 64, COLS)),
            pin(shadow_block.reshape(2, 5, 64, COLS)),
        )
        basis, shadow, moments = pl.pallas_call(
            functools.partial(finish, 1.0 / count),
            out_shape=(field_shape, field_shape, moments_shape),
            in_specs=[anywhere, anywhere, inside],
            out_specs=(anywhere, anywhere, inside),
            scratch_shapes=[pltpu.SemaphoreType.DMA((2,))],
            compiler_params=pltpu.CompilerParams(vmem_limit_bytes=grant),
            name="finish",
        )(*powers)
        return basis.reshape(start_block.shape), shadow.reshape(start_block.shape), moments

    placed = P("sub", "dom", None, None, None)
    return jax.shard_map(
        body,
        mesh=mesh,
        in_specs=(placed, P("sub", "dom", None, None, None, None), placed, placed),
        out_specs=(placed, placed, P()),
        check_vma=False,
    )
```

time: 67.7 us -> 56.1 us (0.83); the launches traced: 66.5 us -> 55.9 us
  local copies, waits for them, and re-layouts: 6.14 us -> 0 us
  Pallas kernels: 59.8 us -> 55.3 us
    unnamed x11 -> x0, local copies, waits for them, and re-layouts: 6.14 us -> none
    pallas_call x1 -> x2, Pallas kernels: 59.8 us -> 55.3 us  [the longest x1 53.8 us: body(): pl.pallas_call(functools.partial(kernel, (doms, subs, depth)), out_shape=...]
where the time goes in v2:
time: 56.1 us; the launch traced here: 55.9 us
  Pallas kernels  55.3 us (99%)
  between operations  0.64 us (1%)
    pallas_call x1, Pallas kernels, body(): pl.pallas_call(functools.partial(kernel, (doms, subs, depth)), out_shape=...  53.8 us
    pallas_call x1, Pallas kernels, body(): pl.pallas_call(functools.partial(finish, 1.0 / count), out_shape=(field_s...  1.46 us

profile of v2, /device:TPU:1, one launch (start us, length us, event | category | flops | bytes accessed | tf_op | source)
XLA Modules:
  0.0 55.9 jit_solution(15846444310001592454)
XLA Ops:
  0.6 53.8 %powers.1 = (f32[2,5,64,128]{3,2,1,0:T(8,128)S(1)}, f32[2,5,64,128]{3,2,1,0:T(8,128)S(1)}, f32[9,128]{1,0:T(8,128)S(1)}) custom-call(f32[2,320,320]{2,1,0:T(8,128)} %bitcast.6, f32[2,3,80,80]{3,2,1,0:T(8,128)} %bitcast.9, f32[2,5,64,128]{3,2,1,0:T(8,128)} %bitcast.7, f32[2,5,64,128]{3,2,1,0:T(8,128)} %bitcast.8), custom_call_target="tpu_custom_call" | custom-call | tf_op jit(solution)/shard_map/powers/pallas_call | solution.py:381
  54.5 1.5 %finish.1 = (f32[2,5,64,128]{3,2,1,0:T(8,128)}, f32[2,5,64,128]{3,2,1,0:T(8,128)}, f32[5,5,128]{2,1,0:T(8,128)}) custom-call(f32[2,5,64,128]{3,2,1,0:T(8,128)S(1)} %get-tuple-element.9.b_hbm, f32[2,5,64,128]{3,2,1,0:T(8,128)S(1)} %get-tuple-element.10.s_hbm, f32[9,128]{1,0:T(8,128)S(1)} %get-tuple-element.11.total_ref), custom_call_target="tpu_custom_call" | custom-call | tf_op jit(solution)/shard_map/finish/pallas_call | solution.py:422

commit v3 on v2

--- a/solution.py
+++ b/solution.py
@@ -14,7 +14,7 @@
 MESH = pl.DeviceIdType.MESH
 F32 = jnp.float32
 BF16 = jnp.bfloat16
-X_DOWN, Y_DOWN, X_UP, Y_UP = range(4)
+DOWN, UP = range(2)
 TOKENS = 6
 SUMS = 2 * STEPS + 1
 
@@ -57,23 +57,23 @@
 
 
 def y_parts(u):
-    parts = u.reshape(20, 4, 8, COLS)
+    parts = u.reshape(10, 4, 8, COLS)
     return [parts[:, i] for i in range(4)]
 
 
 def y_low(u):
     first, _, second, _ = y_parts(u)
-    return jnp.where(low_half(first.shape), first, swap_halves(second)).reshape(2, FACE, COLS)
+    return jnp.where(low_half(first.shape), first, swap_halves(second)).reshape(FACE, COLS)
 
 
 def y_high(u):
     _, first, _, second = y_parts(u)
-    return jnp.where(low_half(first.shape), swap_halves(first), second).reshape(2, FACE, COLS)
+    return jnp.where(low_half(first.shape), swap_halves(first), second).reshape(FACE, COLS)
 
 
 def add_y(u, low, high):
     parts = y_parts(u)
-    low, high = low.reshape(20, 8, COLS), high.reshape(20, 8, COLS)
+    low, high = low.reshape(10, 8, COLS), high.reshape(10, 8, COLS)
     mask = low_half(low.shape)
     zero = jnp.zeros_like(low)
     terms = [
@@ -83,7 +83,7 @@
         jnp.where(mask, zero, high),
     ]
     whole = jnp.concatenate([(part + term)[:, None] for part, term in zip(parts, terms)], axis=1)
-    return whole.reshape(2, 5, 64, COLS)
+    return whole.reshape(5, 64, COLS)
 
 
 def column_sums(x, y):
@@ -113,17 +113,23 @@
     left,
     left_up,
     left_in,
+    left_y,
     right,
     right_up,
     right_in,
-    sent,
-    got,
+    right_y,
+    x_sent,
+    x_got,
+    y_sent,
+    y_got,
     sums,
     sums_got,
     load_sem,
     store_sem,
-    send_sem,
-    recv_sem,
+    x_send,
+    x_recv,
+    y_send,
+    y_recv,
     sums_send,
     sums_recv,
     token_sem,
@@ -136,12 +142,11 @@
 
     loads = [
         pltpu.make_async_copy(b_hbm, field.at[0], load_sem.at[0]),
-        pltpu.make_async_copy(c_hbm, c_in, load_sem.at[1]),
-        pltpu.make_async_copy(s_hbm, field.at[1], load_sem.at[2]),
+        pltpu.make_async_copy(s_hbm, field.at[1], load_sem.at[1]),
+        pltpu.make_async_copy(c_hbm, c_in, load_sem.at[2]),
         pltpu.make_async_copy(d_hbm, d_in, load_sem.at[3]),
     ]
-    for load in loads:
-        load.start()
+    loads[0].start()
 
     def on_sub(by):
         return dom, lax.rem(sub + by + subs, subs)
@@ -158,69 +163,100 @@
     def on_chip(by, to):
         return dom, lax.rem(chip + by, chips) * 2 + to
 
-    sides = [on_sub(-1), on_dom(-1), on_sub(1), on_dom(1)]
     near = [on_level(-1), on_level(1), on_height(-1), on_height(1)]
+    greeted = [on_dom(-1), on_dom(1), on_sub(-1), on_sub(1)] + near
     barrier = pltpu.get_barrier_semaphore()
-    for peer in sides + near:
+    for peer in greeted:
         pl.semaphore_signal(barrier, inc=1, device_id=peer, device_id_type=MESH)
+
+    for load in loads[1:]:
+        load.start()
 
     def pass_token(step):
         for peer in near:
             pl.semaphore_signal(token_sem.at[step], inc=1, device_id=peer, device_id_type=MESH)
 
-    def message(k, f, side):
+    def x_message(k, f, way):
         return pltpu.make_async_remote_copy(
-            src_ref=sent.at[k, f, side],
-            dst_ref=got.at[k, f, side],
-            send_sem=send_sem.at[k, f, side],
-            recv_sem=recv_sem.at[k, f, side],
-            device_id=sides[side],
+            src_ref=x_sent.at[k, f, way],
+            dst_ref=x_got.at[k, f, way],
+            send_sem=x_send.at[k, f, way],
+            recv_sem=x_recv.at[k, f, way],
+            device_id=on_sub(2 * way - 1),
             device_id_type=MESH,
         )
 
-    def through(lefts, side, rights, x):
+    def y_message(k, f, way, e):
+        return pltpu.make_async_remote_copy(
+            src_ref=y_sent.at[k, f, way, e],
+            dst_ref=y_got.at[k, f, way, e],
+            send_sem=y_send.at[k, f, way, e],
+            recv_sem=y_recv.at[k, f, way, e],
+            device_id=on_dom(2 * way - 1),
+            device_id_type=MESH,
+        )
+
+    def through(lefts, e, rights, x):
+        put_columns(rights.at[e], 0, x)
+        return product(lefts[e], rights[e])
+
+    def y_down(k, f, e, trace):
+        y_sent[k, f, DOWN, e] = trace
+        y_message(k, f, DOWN, e).start()
+
+    def y_up(k, f, e):
+        y_sent[k, f, UP, e] = product(left_y[e], right_y[e])
+        y_message(k, f, UP, e).start()
+
+    def x_down(k, f):
+        x_sent[k, f, DOWN] = x_face(field.at[f], 0)
+        x_message(k, f, DOWN).start()
+
+    def x_up(k, f):
+        trace = x_face(field.at[f], 3)
         for e in range(2):
-            put_columns(rights.at[side, e], 0, x[e])
-        parts = [product(lefts[side, e], rights[side, e]) for e in range(2)]
-        return jnp.concatenate([part[None] for part in parts], axis=0)
-
-    for ref in (c_pad, right_up, right_in):
+            x_sent[k, f, UP, e] = through(left_up, e, right_up, trace[e])
+        x_message(k, f, UP).start()
+
+    for ref in (c_pad, right_up, right_in, left_y, right_y):
         ref[...] = jnp.zeros_like(ref)
 
     loads[0].wait()
-    sent[0, 0, Y_DOWN] = y_low(field[0])
-    sent[0, 0, X_DOWN] = x_face(field.at[0], 0)
-    pl.semaphore_wait(barrier, len(sides + near))
-    message(0, 0, Y_DOWN).start()
-    message(0, 0, X_DOWN).start()
+    for e in range(2):
+        y_sent[0, 0, DOWN, e] = y_low(field[0, e])
+    x_sent[0, 0, DOWN] = x_face(field.at[0], 0)
+    pl.semaphore_wait(barrier, len(greeted))
+    for e in range(2):
+        y_message(0, 0, DOWN, e).start()
+    x_message(0, 0, DOWN).start()
     pass_token(0)
-
     loads[1].wait()
+    for e in range(2):
+        y_down(0, 1, e, y_low(field[1, e]))
+    x_down(0, 1)
+
+    loads[2].wait()
     for e in range(2):
         for side, last in enumerate((sub == subs - 1, dom == doms - 1)):
             c_pad[e, side, 0:FACE, 0:FACE] = jnp.where(last, 0.0, c_in[e, side])
         c_pad[e, 2, 0:FACE, 0:FACE] = c_in[e, 2]
-    for side in (1, 0):
+    for e in range(2):
+        put_rows(left_y.at[e], 0, 0, FACE, c_pad[e, 1].T[:FACE])
+    for f in range(2):
         for e in range(2):
-            put_rows(left_up.at[side, e], 0, 0, FACE, c_pad[e, side].T[:FACE])
-
-    def send_up(k, f, side, trace):
-        sent[k, f, X_UP + side] = through(left_up, side, right_up, trace)
-        message(k, f, X_UP + side).start()
-
-    send_up(0, 0, 1, y_high(field[0]))
-    send_up(0, 0, 0, x_face(field.at[0], 3))
-    loads[2].wait()
-    sent[0, 1, Y_DOWN] = y_low(field[1])
-    message(0, 1, Y_DOWN).start()
-    send_up(0, 1, 1, y_high(field[1]))
-    sent[0, 1, X_DOWN] = x_face(field.at[1], 0)
-    message(0, 1, X_DOWN).start()
-    send_up(0, 1, 0, x_face(field.at[1], 3))
+            put_columns(right_y.at[e], 0, y_high(field[f, e]))
+            y_up(0, f, e)
+    for e in range(2):
+        put_rows(left_up.at[e], 0, 0, FACE, c_pad[e, 0].T[:FACE])
+    for f in range(2):
+        x_up(0, f)
 
     for side in range(2):
         for e in range(2):
             put_rows(left_in.at[side, e], 0, 0, FACE, c_pad[e, side, 0:FACE])
+    for e in range(2):
+        put_columns(right_in.at[e], 0, c_pad[e, 1, 0:FACE])
+        put_rows(left_y.at[e], 0, COLS, FACE, product(left_y[e, :, 0:COLS], right_in[e]))
     for ref in (z_pad, d_pad, left, right):
         ref[...] = jnp.zeros_like(ref)
     z_pad[0, pl.ds(3, FACE, stride=4), :] = c_pad[0, 2, 0:FACE]
@@ -250,31 +286,40 @@
     sums[0, 0:1] = column_sums(field[1], field[0])
 
     for k in range(STEPS):
+        more = k + 1 < STEPS
         for f in range(2):
-            more = k + 1 < STEPS
             sign = 1.0 - 2.0 * f
-            message(k, f, X_UP).wait_recv()
-            message(k, f, X_DOWN).wait_recv()
-            into = through(left_in, 0, right_in, got[k, f, X_DOWN]).reshape(2, 5, 16, COLS)
-            acc[f, :, :, 48:64] = acc[f, :, :, 48:64] + sign * into
-            from_below = got[k, f, X_UP].reshape(2, 5, 16, COLS)
-            acc[f, :, :, 0:16] = acc[f, :, :, 0:16] - sign * from_below
-            u = acc[f]
-            message(k, f, Y_UP).wait_recv()
-            low = -sign * got[k, f, Y_UP]
+            for way in (UP, DOWN):
+                x_message(k, f, way).wait_recv()
+            for e in range(2):
+                into = through(left_in.at[0], e, right_in, x_got[k, f, DOWN, e]).reshape(5, 16, COLS)
+                acc[f, e, :, 48:64] = acc[f, e, :, 48:64] + sign * into
+                back = x_got[k, f, UP, e].reshape(5, 16, COLS)
+                acc[f, e, :, 0:16] = acc[f, e, :, 0:16] - sign * back
             if more:
-                sent[k + 1, f, Y_DOWN] = y_low(u) + low
-                message(k + 1, f, Y_DOWN).start()
-            message(k, f, Y_DOWN).wait_recv()
-            high = sign * through(left_in, 1, right_in, got[k, f, Y_DOWN])
+                for e in range(2):
+                    put_columns(right_y.at[e], 0, y_high(acc[f, e]))
+
+            def from_above(e):
+                y_message(k, f, DOWN, e).wait_recv()
+                put_columns(right_y.at[e], COLS, sign * y_got[k, f, DOWN, e])
+                if more:
+                    y_up(k + 1, f, e)
+
+            def from_below(e):
+                y_message(k, f, UP, e).wait_recv()
+                if more:
+                    y_down(k + 1, f, e, y_low(acc[f, e]) - sign * y_got[k, f, UP, e])
+
+            for e in range(2):
+                from_below(e)
+                from_above(e)
+            for e in range(2):
+                high = product(left_in[1, e], right_y[e, COLS:])
+                field[f, e] = add_y(acc[f, e], -sign * y_got[k, f, UP, e], high)
             if more:
-                send_up(k + 1, f, 1, y_high(u) + high)
-            field[f] = add_y(u, low, high)
-            if more:
-                sent[k + 1, f, X_DOWN] = x_face(field.at[f], 0)
-                message(k + 1, f, X_DOWN).start()
-                send_up(k + 1, f, 0, x_face(field.at[f], 3))
-                local_part(f)
+                x_down(k + 1, f)
+                x_up(k + 1, f)
             else:
                 pltpu.make_async_copy(field.at[f], (ob_hbm, os_hbm)[f], store_sem.at[f]).start()
             moment = 2 * k + 1 + f
@@ -284,6 +329,9 @@
                 pl.semaphore_wait(token_sem.at[step], len(near))
                 if step + 1 < TOKENS:
                     pass_token(step + 1)
+            if more and f == 1:
+                local_part(0)
+                local_part(1)
 
     def total_copy(stage, slot, peer, send=None):
         return pltpu.make_async_remote_copy(
@@ -329,9 +377,12 @@
             copy.start()
         sums[2] = arrived(sums[1], 1, slot_y, heights - 1)
         along_z = []
-        for i, by in enumerate(far_first(depth)):
-            along_z.append(total_copy(2, slot_z + i, on_level(by, chip * 2), slot_out + 1 + i))
-            along_z.append(total_copy(2, slot_z + i, on_level(by)))
+        for i in range(depth - 1):
+            after = (i + depth - level) // depth
+            place = height * depth + i + after
+            slot = slot_z + level - 1 + after
+            along_z.append(total_copy(2, slot, (place, chip * 2), slot_z + i))
+            along_z.append(total_copy(2, slot, (place, sub), slot_out + 1 + i))
         along_z.append(total_copy(2, slot_out, inner))
         for copy in along_z:
             copy.start()
@@ -341,8 +392,10 @@
 
     for k in range(STEPS):
         for f in range(2):
-            for side in range(4):
-                message(k, f, side).wait_send()
+            for way in range(2):
+                x_message(k, f, way).wait_send()
+                for e in range(2):
+                    y_message(k, f, way, e).wait_send()
     for f in range(2):
         pltpu.make_async_copy(field.at[f], (ob_hbm, os_hbm)[f], store_sem.at[f]).wait()
 
@@ -353,9 +406,8 @@
 
 def finish(scale, b_hbm, s_hbm, total_ref, ob_hbm, os_hbm, moments_ref, sem):
     copies = [
-        pltpu.make_async_copy(b_hbm, ob_hbm, sem.at[0]),
-        pltpu.make_async_copy(s_hbm, os_hbm, sem.at[1]),
-    ]
+        pltpu.make_async_copy(b_hbm.at[e], ob_hbm.at[e], sem.at[0, e]) for e in range(2)
+    ] + [pltpu.make_async_copy(s_hbm.at[e], os_hbm.at[e], sem.at[1, e]) for e in range(2)]
     for copy in copies:
         copy.start()
     total = total_ref[...] * scale
@@ -392,19 +444,22 @@
                 pltpu.VMEM((2, 3, COLS, COLS), F32),
                 pltpu.VMEM((2, ROWS, COLS), F32),
                 pltpu.VMEM((2, 2, 2 * ROWS, 512), BF16),
+                pltpu.VMEM((2, 2 * FACE, COLS), BF16),
                 pltpu.VMEM((2, 2, 2 * FACE, COLS), BF16),
-                pltpu.VMEM((2, 2, 2 * FACE, COLS), BF16),
+                pltpu.VMEM((2, 2 * FACE, 256), BF16),
                 pltpu.VMEM((2, 512, 256), BF16),
-                pltpu.VMEM((2, 2, COLS, 256), BF16),
-                pltpu.VMEM((2, 2, COLS, 256), BF16),
-                pltpu.VMEM((STEPS, 2, 4, 2, FACE, COLS), F32),
-                pltpu.VMEM((STEPS, 2, 4, 2, FACE, COLS), F32),
+                pltpu.VMEM((2, COLS, 256), BF16),
+                pltpu.VMEM((2, COLS, 256), BF16),
+                pltpu.VMEM((2, 256, 256), BF16),
+                *[pltpu.VMEM((STEPS, 2, 2, 2, FACE, COLS), F32)] * 4,
                 pltpu.VMEM((3, SUMS, COLS), F32),
                 pltpu.VMEM((slots, SUMS, COLS), F32),
                 pltpu.SemaphoreType.DMA((4,)),
                 pltpu.SemaphoreType.DMA((2,)),
-                pltpu.SemaphoreType.DMA((STEPS, 2, 4)),
-                pltpu.SemaphoreType.DMA((STEPS, 2, 4)),
+                pltpu.SemaphoreType.DMA((STEPS, 2, 2)),
+                pltpu.SemaphoreType.DMA((STEPS, 2, 2)),
+                pltpu.SemaphoreType.DMA((STEPS, 2, 2, 2)),
+                pltpu.SemaphoreType.DMA((STEPS, 2, 2, 2)),
                 pltpu.SemaphoreType.DMA((slots + depth - 1,)),
                 pltpu.SemaphoreType.DMA((slots,)),
                 pltpu.SemaphoreType.REGULAR((TOKENS,)),
@@ -424,7 +479,7 @@
             out_shape=(field_shape, field_shape, moments_shape),
             in_specs=[anywhere, anywhere, inside],
             out_specs=(anywhere, anywhere, inside),
-            scratch_shapes=[pltpu.SemaphoreType.DMA((2,))],
+            scratch_shapes=[pltpu.SemaphoreType.DMA((2, 2))],
             compiler_params=pltpu.CompilerParams(vmem_limit_bytes=grant),
             name="finish",
         )(*powers)

time: 56.1 us -> 54 us (0.963)
  Pallas kernels: 55.3 us -> 53.2 us
    pallas_call x1, Pallas kernels: 53.8 us -> 51.7 us  [body(): pl.pallas_call(functools.partial(kernel, (doms, subs, depth)), out_shape=...]
where the time goes in v3:
time: 54 us; the launch traced here: 53.8 us
  Pallas kernels  53.2 us (99%)
  between operations  0.64 us (1%)
    pallas_call x1, Pallas kernels, body(): pl.pallas_call(functools.partial(kernel, (doms, subs, depth)), out_shape=...  51.7 us
    pallas_call x1, Pallas kernels, body(): pl.pallas_call(functools.partial(finish, 1.0 / count), out_shape=(field_s...  1.47 us

profile of v3, /device:TPU:1, one launch (start us, length us, event | category | flops | bytes accessed | tf_op | source)
XLA Modules:
  0.0 53.8 jit_solution(10459234281556334451)
XLA Ops:
  0.6 51.7 %powers.1 = (f32[2,5,64,128]{3,2,1,0:T(8,128)S(1)}, f32[2,5,64,128]{3,2,1,0:T(8,128)S(1)}, f32[9,128]{1,0:T(8,128)S(1)}) custom-call(f32[2,320,320]{2,1,0:T(8,128)} %bitcast.6, f32[2,3,80,80]{3,2,1,0:T(8,128)} %bitcast.9, f32[2,5,64,128]{3,2,1,0:T(8,128)} %bitcast.7, f32[2,5,64,128]{3,2,1,0:T(8,128)} %bitcast.8), custom_call_target="tpu_custom_call" | custom-call | tf_op jit(solution)/shard_map/powers/pallas_call | solution.py:433
  52.3 1.5 %finish.1 = (f32[2,5,64,128]{3,2,1,0:T(8,128)}, f32[2,5,64,128]{3,2,1,0:T(8,128)}, f32[5,5,128]{2,1,0:T(8,128)}) custom-call(f32[2,5,64,128]{3,2,1,0:T(8,128)S(1)} %get-tuple-element.9.b_hbm, f32[2,5,64,128]{3,2,1,0:T(8,128)S(1)} %get-tuple-element.10.s_hbm, f32[9,128]{1,0:T(8,128)S(1)} %get-tuple-element.11.total_ref), custom_call_target="tpu_custom_call" | custom-call | tf_op jit(solution)/shard_map/finish/pallas_call | solution.py:477

commit v4 on v3

--- a/solution.py
+++ b/solution.py
@@ -141,12 +141,13 @@
     chip, core = sub // 2, lax.rem(sub, 2)
 
     loads = [
-        pltpu.make_async_copy(b_hbm, field.at[0], load_sem.at[0]),
-        pltpu.make_async_copy(s_hbm, field.at[1], load_sem.at[1]),
-        pltpu.make_async_copy(c_hbm, c_in, load_sem.at[2]),
+        pltpu.make_async_copy(c_hbm, c_in, load_sem.at[0]),
+        pltpu.make_async_copy(b_hbm, field.at[0], load_sem.at[1]),
+        pltpu.make_async_copy(s_hbm, field.at[1], load_sem.at[2]),
         pltpu.make_async_copy(d_hbm, d_in, load_sem.at[3]),
     ]
     loads[0].start()
+    loads[1].start()
 
     def on_sub(by):
         return dom, lax.rem(sub + by + subs, subs)
@@ -169,7 +170,7 @@
     for peer in greeted:
         pl.semaphore_signal(barrier, inc=1, device_id=peer, device_id_type=MESH)
 
-    for load in loads[1:]:
+    for load in loads[2:]:
         load.start()
 
     def pass_token(step):
@@ -223,33 +224,37 @@
 
     loads[0].wait()
     for e in range(2):
-        y_sent[0, 0, DOWN, e] = y_low(field[0, e])
-    x_sent[0, 0, DOWN] = x_face(field.at[0], 0)
-    pl.semaphore_wait(barrier, len(greeted))
-    for e in range(2):
-        y_message(0, 0, DOWN, e).start()
-    x_message(0, 0, DOWN).start()
-    pass_token(0)
-    loads[1].wait()
-    for e in range(2):
-        y_down(0, 1, e, y_low(field[1, e]))
-    x_down(0, 1)
-
-    loads[2].wait()
-    for e in range(2):
         for side, last in enumerate((sub == subs - 1, dom == doms - 1)):
             c_pad[e, side, 0:FACE, 0:FACE] = jnp.where(last, 0.0, c_in[e, side])
         c_pad[e, 2, 0:FACE, 0:FACE] = c_in[e, 2]
     for e in range(2):
         put_rows(left_y.at[e], 0, 0, FACE, c_pad[e, 1].T[:FACE])
-    for f in range(2):
-        for e in range(2):
+        put_rows(left_up.at[e], 0, 0, FACE, c_pad[e, 0].T[:FACE])
+
+    def first_traces(f):
+        loads[1 + f].wait()
+        for e in range(2):
+            y_sent[0, f, DOWN, e] = y_low(field[f, e])
             put_columns(right_y.at[e], 0, y_high(field[f, e]))
-            y_up(0, f, e)
-    for e in range(2):
-        put_rows(left_up.at[e], 0, 0, FACE, c_pad[e, 0].T[:FACE])
-    for f in range(2):
-        x_up(0, f)
+            y_sent[0, f, UP, e] = product(left_y[e], right_y[e])
+        x_sent[0, f, DOWN] = x_face(field.at[f], 0)
+        trace = x_face(field.at[f], 3)
+        for e in range(2):
+            x_sent[0, f, UP, e] = through(left_up, e, right_up, trace[e])
+
+    def first_sends(f):
+        for e in range(2):
+            for way in range(2):
+                y_message(0, f, way, e).start()
+        for way in range(2):
+            x_message(0, f, way).start()
+
+    first_traces(0)
+    first_traces(1)
+    pl.semaphore_wait(barrier, len(greeted))
+    first_sends(0)
+    first_sends(1)
+    pass_token(0)
 
     for side in range(2):
         for e in range(2):
@@ -355,26 +360,42 @@
     slot_z = slot_y + heights - 1
     slot_out = slot_z + depth - 1
 
+    def settle():
+        for k in range(STEPS):
+            for f in range(2):
+                for way in range(2):
+                    x_message(k, f, way).wait_send()
+                    for e in range(2):
+                        y_message(k, f, way, e).wait_send()
+        for f in range(2):
+            pltpu.make_async_copy(field.at[f], (ob_hbm, os_hbm)[f], store_sem.at[f]).wait()
+
     @pl.when(core == 0)
     def _():
         copies = [total_copy(0, i, on_chip(by, 1)) for i, by in enumerate(across)]
         copies.append(total_copy(0, slot_in, outer))
         for copy in copies:
             copy.start()
+        settle()
+        for copy in copies:
+            copy.wait_send()
         total_copy(2, slot_out, outer).wait_recv()
         total_ref[...] = arrived(sums_got[slot_out], 2, slot_z, depth - 1)
-        for copy in copies:
-            copy.wait_send()
 
     @pl.when(core == 1)
     def _():
         copies = [total_copy(0, len(across) + i, on_chip(by, 1)) for i, by in enumerate(across)]
         for copy in copies:
             copy.start()
+        settle()
+        for copy in copies:
+            copy.wait_send()
         sums[1] = arrived(sums[0], 0, 0, slot_y)
         along_y = [total_copy(1, slot_y + i, on_height(by)) for i, by in enumerate(far_first(heights))]
         for copy in along_y:
             copy.start()
+        for copy in along_y:
+            copy.wait_send()
         sums[2] = arrived(sums[1], 1, slot_y, heights - 1)
         along_z = []
         for i in range(depth - 1):
@@ -386,25 +407,16 @@
         along_z.append(total_copy(2, slot_out, inner))
         for copy in along_z:
             copy.start()
+        for copy in along_z:
+            copy.wait_send()
         total_ref[...] = arrived(sums[2], 2, slot_z, depth - 1)
-        for copy in copies + along_y + along_z:
-            copy.wait_send()
-
-    for k in range(STEPS):
-        for f in range(2):
-            for way in range(2):
-                x_message(k, f, way).wait_send()
-                for e in range(2):
-                    y_message(k, f, way, e).wait_send()
-    for f in range(2):
-        pltpu.make_async_copy(field.at[f], (ob_hbm, os_hbm)[f], store_sem.at[f]).wait()
 
 
 def pin(x):
     return pltpu.with_memory_space_constraint(x, pltpu.HBM)
 
 
-def finish(scale, b_hbm, s_hbm, total_ref, ob_hbm, os_hbm, moments_ref, sem):
+def finish(scale, b_hbm, s_hbm, total_ref, ob_hbm, os_hbm, moments_hbm, moments_ref, moments_sem, sem):
     copies = [
         pltpu.make_async_copy(b_hbm.at[e], ob_hbm.at[e], sem.at[0, e]) for e in range(2)
     ] + [pltpu.make_async_copy(s_hbm.at[e], os_hbm.at[e], sem.at[1, e]) for e in range(2)]
@@ -413,6 +425,8 @@
     total = total_ref[...] * scale
     for i in range(STEPS + 1):
         moments_ref[i] = total[i : i + STEPS + 1]
+    copies.append(pltpu.make_async_copy(moments_ref, moments_hbm, moments_sem))
+    copies[-1].start()
     for copy in copies:
         copy.wait()
 
@@ -478,8 +492,8 @@
             functools.partial(finish, 1.0 / count),
             out_shape=(field_shape, field_shape, moments_shape),
             in_specs=[anywhere, anywhere, inside],
-            out_specs=(anywhere, anywhere, inside),
-            scratch_shapes=[pltpu.SemaphoreType.DMA((2, 2))],
+            out_specs=(anywhere, anywhere, anywhere),
+            scratch_shapes=[pltpu.VMEM((STEPS + 1, STEPS + 1, COLS), F32), pltpu.SemaphoreType.DMA, pltpu.SemaphoreType.DMA((2, 2))],
             compiler_params=pltpu.CompilerParams(vmem_limit_bytes=grant),
             name="finish",
         )(*powers)

time: 54 us -> 53.2 us (0.985)
  Pallas kernels: 53.2 us -> 52.4 us
    pallas_call x1, Pallas kernels: 1.47 us -> 0.88 us  [body(): pl.pallas_call(functools.partial(finish, 1.0 / count), out_shape=(field_s...]
where the time goes in v4:
time: 53.2 us; the launch traced here: 53.1 us
  Pallas kernels  52.4 us (98%)
  between operations  0.64 us (1%)
    pallas_call x1, Pallas kernels, body(): pl.pallas_call(functools.partial(kernel, (doms, subs, depth)), out_shape=...  51.5 us

profile of v4, /device:TPU:1, one launch (start us, length us, event | category | flops | bytes accessed | tf_op | source)
XLA Modules:
  0.0 53.1 jit_solution(17441763425865777642)
XLA Ops:
  0.6 51.5 %powers.1 = (f32[2,5,64,128]{3,2,1,0:T(8,128)S(1)}, f32[2,5,64,128]{3,2,1,0:T(8,128)S(1)}, f32[9,128]{1,0:T(8,128)S(1)}) custom-call(f32[2,320,320]{2,1,0:T(8,128)} %bitcast.6, f32[2,3,80,80]{3,2,1,0:T(8,128)} %bitcast.9, f32[2,5,64,128]{3,2,1,0:T(8,128)} %bitcast.7, f32[2,5,64,128]{3,2,1,0:T(8,128)} %bitcast.8), custom_call_target="tpu_custom_call" | custom-call | tf_op jit(solution)/shard_map/powers/pallas_call | solution.py:447
  52.2 0.9 %finish.1 = (f32[2,5,64,128]{3,2,1,0:T(8,128)}, f32[2,5,64,128]{3,2,1,0:T(8,128)}, f32[5,5,128]{2,1,0:T(8,128)}) custom-call(f32[2,5,64,128]{3,2,1,0:T(8,128)S(1)} %get-tuple-element.9.b_hbm, f32[2,5,64,128]{3,2,1,0:T(8,128)S(1)} %get-tuple-element.10.s_hbm, f32[9,128]{1,0:T(8,128)S(1)} %get-tuple-element.11.total_ref), custom_call_target="tpu_custom_call" | custom-call | tf_op jit(solution)/shard_map/finish/pallas_call | solution.py:491

commit v5 on v4

--- a/solution.py
+++ b/solution.py
@@ -87,7 +87,7 @@
 
 
 def column_sums(x, y):
-    return jnp.sum((x * y).reshape(2 * ROWS, COLS), axis=0, keepdims=True)
+    return jnp.sum((x * y).reshape(-1, COLS), axis=0, keepdims=True)
 
 
 def far_first(count):
@@ -316,19 +316,23 @@
                 if more:
                     y_down(k + 1, f, e, y_low(acc[f, e]) - sign * y_got[k, f, UP, e])
 
+            def update(e):
+                high = product(left_in[1, e], right_y[e, COLS:])
+                field[f, e] = add_y(acc[f, e], -sign * y_got[k, f, UP, e], high)
+                return column_sums(field[1, e], field[0, e])
+
+            parts = []
             for e in range(2):
                 from_below(e)
                 from_above(e)
-            for e in range(2):
-                high = product(left_in[1, e], right_y[e, COLS:])
-                field[f, e] = add_y(acc[f, e], -sign * y_got[k, f, UP, e], high)
+                parts.append(update(e))
             if more:
                 x_down(k + 1, f)
                 x_up(k + 1, f)
             else:
                 pltpu.make_async_copy(field.at[f], (ob_hbm, os_hbm)[f], store_sem.at[f]).start()
             moment = 2 * k + 1 + f
-            sums[0, moment : moment + 1] = column_sums(field[1], field[0])
+            sums[0, moment : moment + 1] = parts[0] + parts[1]
             step = 2 * k + f
             if step < TOKENS:
                 pl.semaphore_wait(token_sem.at[step], len(near))

time: 53.2 us -> 53.1 us (level)
  no operation moved by 1% of the time
where the time goes in v5:
time: 53.1 us; the launch traced here: 52.9 us
  Pallas kernels  52.3 us (98%)
  between operations  0.64 us (1%)
    pallas_call x1, Pallas kernels, body(): pl.pallas_call(functools.partial(kernel, (doms, subs, depth)), out_shape=...  51.4 us

profile of v5, /device:TPU:1, one launch (start us, length us, event | category | flops | bytes accessed | tf_op | source)
XLA Modules:
  0.0 52.9 jit_solution(17218396679429315676)
XLA Ops:
  0.6 51.4 %powers.1 = (f32[2,5,64,128]{3,2,1,0:T(8,128)S(1)}, f32[2,5,64,128]{3,2,1,0:T(8,128)S(1)}, f32[9,128]{1,0:T(8,128)S(1)}) custom-call(f32[2,320,320]{2,1,0:T(8,128)} %bitcast.6, f32[2,3,80,80]{3,2,1,0:T(8,128)} %bitcast.9, f32[2,5,64,128]{3,2,1,0:T(8,128)} %bitcast.7, f32[2,5,64,128]{3,2,1,0:T(8,128)} %bitcast.8), custom_call_target="tpu_custom_call" | custom-call | tf_op jit(solution)/shard_map/powers/pallas_call | solution.py:451
  52.0 0.9 %finish.1 = (f32[2,5,64,128]{3,2,1,0:T(8,128)}, f32[2,5,64,128]{3,2,1,0:T(8,128)}, f32[5,5,128]{2,1,0:T(8,128)}) custom-call(f32[2,5,64,128]{3,2,1,0:T(8,128)S(1)} %get-tuple-element.9.b_hbm, f32[2,5,64,128]{3,2,1,0:T(8,128)S(1)} %get-tuple-element.10.s_hbm, f32[9,128]{1,0:T(8,128)S(1)} %get-tuple-element.11.total_ref), custom_call_target="tpu_custom_call" | custom-call | tf_op jit(solution)/shard_map/finish/pallas_call | solution.py:495

commit v6 on v5

--- a/solution.py
+++ b/solution.py
@@ -329,8 +329,8 @@
             if more:
                 x_down(k + 1, f)
                 x_up(k + 1, f)
-            else:
-                pltpu.make_async_copy(field.at[f], (ob_hbm, os_hbm)[f], store_sem.at[f]).start()
+            elif f == 0:
+                pltpu.make_async_copy(field.at[0], ob_hbm, store_sem.at[0]).start()
             moment = 2 * k + 1 + f
             sums[0, moment : moment + 1] = parts[0] + parts[1]
             step = 2 * k + f
@@ -365,6 +365,7 @@
     slot_out = slot_z + depth - 1
 
     def settle():
+        pltpu.make_async_copy(field.at[1], os_hbm, store_sem.at[1]).start()
         for k in range(STEPS):
             for f in range(2):
                 for way in range(2):

time: 53.1 us -> 52.9 us (level)
  no operation moved by 1% of the time
where the time goes in v6:
time: 52.9 us; the launch traced here: 52.8 us
  Pallas kernels  52.2 us (99%)
  between operations  0.64 us (1%)
    pallas_call x1, Pallas kernels, body(): pl.pallas_call(functools.partial(kernel, (doms, subs, depth)), out_shape=...  51.3 us

profile of v6, /device:TPU:1, one launch (start us, length us, event | category | flops | bytes accessed | tf_op | source)
XLA Modules:
  0.0 52.8 jit_solution(8224677310388365593)
XLA Ops:
  0.6 51.3 %powers.1 = (f32[2,5,64,128]{3,2,1,0:T(8,128)S(1)}, f32[2,5,64,128]{3,2,1,0:T(8,128)S(1)}, f32[9,128]{1,0:T(8,128)S(1)}) custom-call(f32[2,320,320]{2,1,0:T(8,128)} %bitcast.6, f32[2,3,80,80]{3,2,1,0:T(8,128)} %bitcast.9, f32[2,5,64,128]{3,2,1,0:T(8,128)} %bitcast.7, f32[2,5,64,128]{3,2,1,0:T(8,128)} %bitcast.8), custom_call_target="tpu_custom_call" | custom-call | tf_op jit(solution)/shard_map/powers/pallas_call | solution.py:452
  51.9 0.9 %finish.1 = (f32[2,5,64,128]{3,2,1,0:T(8,128)}, f32[2,5,64,128]{3,2,1,0:T(8,128)}, f32[5,5,128]{2,1,0:T(8,128)}) custom-call(f32[2,5,64,128]{3,2,1,0:T(8,128)S(1)} %get-tuple-element.9.b_hbm, f32[2,5,64,128]{3,2,1,0:T(8,128)S(1)} %get-tuple-element.10.s_hbm, f32[9,128]{1,0:T(8,128)S(1)} %get-tuple-element.11.total_ref), custom_call_target="tpu_custom_call" | custom-call | tf_op jit(solution)/shard_map/finish/pallas_call | solution.py:496
